TPU v7x, 512 devices: a whole 4x8x8 slice. The times are simulated.
512 devices in a mesh: wide: 32 (over y, x), narrow: 16 (over z, core).
Axes of the slice: x: 4, y: 8, z: 8, core: 2. Of those that a mesh axis runs over, the one named last changes fastest.
Arguments:
- queries: bfloat16 [65536, 768], P(('wide', 'narrow')), may hold values from -8 to 8
- keys: bfloat16 [65536, 768], P(('wide', 'narrow')), may hold values from -8 to 8
- values: bfloat16 [65536, 768], P(('wide', 'narrow')), may hold values from -6 to 6
- slide_ids: int32 [65536], P(('wide', 'narrow')), may hold values from 0 to 15, never falling along the last dimension, each value on 1 to 12288 neighbouring positions
- w_out: bfloat16 [768, 768], replicated, may hold values from -0.21875 to 0.21875
Outputs:
- encoded: bfloat16 [65536, 768], P(('wide', 'narrow'))
Inputs may be any that keep to these rules, and one draw needn't show every extreme that they name: `slide_ids`: slide numbers never fall along the tokens; each slide holds 1 to 12288 tokens, one exactly 12288.
All inputs are finite; a program needn't handle non-finite values.
Results may differ from a plain program's by a relative error of at most 0.0055.
Values may be sent and summed in bfloat16 or wider, within the bound.
A program may use at most 64 MiB of HBM per device.

v0:
```python
from functools import reduce

import jax
import jax.numpy as jnp
from jax import lax
from jax.sharding import PartitionSpec as P

HEADS = 12
HDIM = 64
RATE_NEAR = 4
RATE_FAR = 8
SEG_LIMIT = 16384


NEG_FILL = -1e30


def from_partner(block, axis, distance):
    count = lax.axis_size(axis)
    route = []
    for low in range(count):
        high = low | 1 << distance
        if high != low and high < count:
            route += [(low, high), (high, low)]
    return lax.ppermute(block, axis, route)


def for_sending(shard):
    return jax.tree.map(lambda a: a.astype(jnp.bfloat16) if a.dtype == jnp.float32 else a, shard)


def pick(source, dilation):
    length = source.shape[0]
    head_ids = jnp.arange(HEADS)
    return source.reshape(length // dilation, dilation, HEADS, HDIM)[
        :, head_ids % dilation, head_ids, :
    ]


def attend(query_rows, query_ids, key_rows, value_rows, key_ids):
    pieces = []
    for first in range(0, HEADS, 4):
        last = first + 4
        scores = jnp.einsum(
            "qhd,khd->hqk",
            query_rows[:, first:last],
            key_rows[:, first:last],
            preferred_element_type=jnp.float32,
        ) * HDIM ** (-0.5)
        same = query_ids[:, first:last].T[:, :, None] == key_ids[:, first:last].T[:, None, :]
        scores = jnp.where(same, scores, NEG_FILL)
        maxima = jnp.max(scores, axis=-1)
        weights = jnp.where(same, jnp.exp(scores - maxima[..., None]), 0.0)
        totals = jnp.sum(weights, axis=-1)
        summed = jnp.einsum(
            "hqk,khd->qhd",
            weights.astype(jnp.bfloat16),
            value_rows[:, first:last],
            preferred_element_type=jnp.float32,
        )
        pieces.append((maxima.T, totals.T, summed))
    return tuple(
        (jnp.concatenate([piece[index] for piece in pieces], axis=1) for index in range(3))
    )


def spread(part, dilation):
    head_ids = jnp.arange(HEADS)
    result = []
    for member, filler in zip(part, (NEG_FILL, 0.0, 0.0)):
        filled = jnp.full((member.shape[0], dilation) + member.shape[1:], filler, member.dtype)
        filled = filled.at[:, head_ids % dilation, head_ids].set(member)
        result.append(filled.reshape((member.shape[0] * dilation,) + member.shape[1:]))
    return tuple(result)


def combine(parts):
    top = reduce(jnp.maximum, [member[0] for member in parts])
    totals = reduce(jnp.add, [member[1] * jnp.exp(member[0] - top) for member in parts])
    numer = reduce(jnp.add, [member[2] * jnp.exp(member[0] - top)[..., None] for member in parts])
    return (numer / totals[..., None]).reshape(numer.shape[0], -1).astype(jnp.bfloat16)


def merge_pair(first, second):
    top = jnp.maximum(first[0], second[0])
    scale_a = jnp.exp(first[0] - top)
    scale_b = jnp.exp(second[0] - top)
    return (
        top,
        first[1] * scale_a + second[1] * scale_b,
        first[2] * scale_a[..., None] + second[2] * scale_b[..., None],
    )


def upper_flag(bit):
    return lax.axis_index("wide") >> bit & 1 == 1


def join_sets(mine, theirs, flag):
    return tuple(
        (
            jnp.concatenate([jnp.where(flag, other, own), jnp.where(flag, own, other)], axis=0)
            for own, other in zip(mine, theirs)
        )
    )


def split_sets(part, flag):
    half = part[0].shape[0] // 2
    keep = tuple((jnp.where(flag, member[half:], member[:half]) for member in part))
    send = tuple((jnp.where(flag, member[:half], member[half:]) for member in part))
    return (keep, send)


def fold_near(part, bits):
    width = HEADS * HDIM
    for bit in reversed(range(bits)):
        keep, send = split_sets(part, upper_flag(bit))
        half = keep[0].shape[0]
        got_max, got_total, got_sum = from_partner(
            (send[0], send[1], send[2].reshape(half, width)), "wide", bit
        )
        part = merge_pair(keep, (got_max, got_total, got_sum.reshape(half, HEADS, HDIM)))
    return part


def fold_far(part, bits):
    width = HEADS * HDIM
    for bit in reversed(range(bits)):
        keep, send = split_sets(part, upper_flag(bit))
        half = keep[0].shape[0]
        got_max, got_total, got_sum = from_partner(
            (send[0], send[1], send[2].reshape(half, width)), "wide", bit
        )
        part = merge_pair(keep, (got_max, got_total, got_sum.reshape(half, HEADS, HDIM)))
    return part


def local(queries, keys, values, slide_ids, w_out):
    count = queries.shape[0]
    width = HEADS * HDIM
    head_ids = jnp.arange(HEADS)
    group_tokens = count * lax.axis_size("narrow")
    near_span = min(SEG_LIMIT, group_tokens * lax.axis_size("wide") // 4)
    near_bits = (near_span // group_tokens).bit_length() - 1
    far_bits = near_bits + 2
    local_ids = jnp.broadcast_to(slide_ids[:, None], (count, HEADS))
    parts = [
        attend(
            queries.reshape(count, HEADS, HDIM),
            local_ids,
            keys.reshape(count, HEADS, HDIM),
            values.reshape(count, HEADS, HDIM),
            local_ids,
        )
    ]
    near_count = count // RATE_NEAR
    near_ids = slide_ids.reshape(near_count, RATE_NEAR)
    near_keys, near_values, near_slides = (
        lax.all_gather(
            pick(keys, RATE_NEAR).reshape(near_count, width), "narrow", axis=0, tiled=True
        ),
        lax.all_gather(
            pick(values, RATE_NEAR).reshape(near_count, width), "narrow", axis=0, tiled=True
        ),
        lax.all_gather(near_ids, "narrow", axis=0, tiled=True),
    )
    near_rows = near_keys.shape[0]
    near_sets = (pick(queries, RATE_NEAR).reshape(near_count, width), near_ids)
    for bit in range(near_bits):
        theirs = jax.tree.map(
            lambda part, own: part.astype(own.dtype),
            from_partner(for_sending(near_sets), "wide", bit),
            near_sets,
        )
        near_sets = join_sets(near_sets, theirs, upper_flag(bit))
    near_total = near_sets[0].shape[0]
    near_part = attend(
        near_sets[0].reshape(near_total, HEADS, HDIM),
        near_sets[1][:, head_ids % RATE_NEAR],
        near_keys.reshape(near_rows, HEADS, HDIM),
        near_values.reshape(near_rows, HEADS, HDIM),
        near_slides[:, head_ids % RATE_NEAR],
    )
    parts.append(spread(fold_near(near_part, near_bits), RATE_NEAR))
    far_count = count // RATE_FAR
    own_flat_keys, own_flat_values, own_slides = (
        lax.all_gather(
            pick(keys, RATE_FAR).reshape(far_count, width), "narrow", axis=0, tiled=True
        ),
        lax.all_gather(
            pick(values, RATE_FAR).reshape(far_count, width), "narrow", axis=0, tiled=True
        ),
        lax.all_gather(slide_ids.reshape(far_count, RATE_FAR), "narrow", axis=0, tiled=True),
    )
    own_rows = own_flat_keys.shape[0]
    own_keys = own_flat_keys.reshape(own_rows, HEADS, HDIM)
    own_values = own_flat_values.reshape(own_rows, HEADS, HDIM)
    far_sets = (
        pick(queries, RATE_FAR).reshape(far_count, width),
        slide_ids.reshape(far_count, RATE_FAR),
    )
    start_bit = 0
    for bit in range(start_bit, far_bits):
        theirs = jax.tree.map(
            lambda part, own: part.astype(own.dtype),
            from_partner(for_sending(far_sets), "wide", bit),
            far_sets,
        )
        far_sets = join_sets(far_sets, theirs, upper_flag(bit))
    far_total = far_sets[0].shape[0]
    far_part = attend(
        far_sets[0].reshape(far_total, HEADS, HDIM),
        far_sets[1][:, head_ids % RATE_FAR],
        own_keys,
        own_values,
        own_slides[:, head_ids % RATE_FAR],
    )
    parts.append(spread(fold_far(far_part, far_bits), RATE_FAR))
    attended = combine(parts)
    return jnp.dot(attended, w_out, preferred_element_type=jnp.float32).astype(jnp.bfloat16)


def solution(mesh):
    placed = (
        P(("wide", "narrow"), None),
        P(("wide", "narrow"), None),
        P(("wide", "narrow"), None),
        P(("wide", "narrow")),
        P(),
    )
    return jax.shard_map(
        local, mesh=mesh, in_specs=placed, out_specs=P(("wide", "narrow"), None), check_vma=False
    )
```

profile of v0, /device:TPU:8, one launch (start us, length us, event | category | flops | bytes accessed | tf_op | source)
XLA Modules:
  0.0 415.5 jit_solution(136553844294839944)
XLA Ops:
  39.3 23.2 %all-gather = s32[16,32,4]{1,2,0:T(4,128)S(1)} all-gather(s32[1,32,4]{1,2,0:T(4,128)S(1)} %copy.195), channel_id=1, replica_groups=mesh['wide'=32,'narrow'=16] {'narrow'}, dimensions={0}, use_global_device_ids=true | all-gather | bytes 8704 | tf_op jit(solution)/shard_map/all_gather | solution.py:166
  67.3 16.9 %all_gather.19 = bf16[512,768]{1,0:T(8,128)(2,1)S(1)} all-gather(bf16[32,768]{1,0:T(8,128)(2,1)} %reshape.415), channel_id=1, replica_groups=mesh['wide'=32,'narrow'=16] {'narrow'}, dimensions={0}, use_global_device_ids=true | all-gather | bytes 835584 | tf_op jit(solution)/shard_map/all_gather | solution.py:160
  86.4 17.9 %all_gather.22 = bf16[512,768]{1,0:T(8,128)(2,1)S(1)} all-gather(bf16[32,768]{1,0:T(8,128)(2,1)S(1)} %reshape.427), channel_id=1, replica_groups=mesh['wide'=32,'narrow'=16] {'narrow'}, dimensions={0}, use_global_device_ids=true | all-gather | bytes 835584 | tf_op jit(solution)/shard_map/all_gather | solution.py:163
  105.6 14.7 %all-gather.1 = s32[16,16,8]{1,2,0:T(8,128)S(1)} all-gather(s32[1,16,8]{1,2,0:T(8,128)S(1)} %copy.208), channel_id=1, replica_groups=mesh['wide'=32,'narrow'=16] {'narrow'}, dimensions={0}, use_global_device_ids=true | all-gather | bytes 8704 | tf_op jit(solution)/shard_map/all_gather | solution.py:194
  122.5 16.8 %all_gather.21 = bf16[256,768]{1,0:T(8,128)(2,1)S(1)} all-gather(bf16[16,768]{1,0:T(8,128)(2,1)S(1)} %reshape.423), channel_id=1, replica_groups=mesh['wide'=32,'narrow'=16] {'narrow'}, dimensions={0}, use_global_device_ids=true | all-gather | bytes 417792 | tf_op jit(solution)/shard_map/all_gather | solution.py:188
  140.4 15.6 %all_gather.23 = bf16[256,768]{1,0:T(8,128)(2,1)S(1)} all-gather(bf16[16,768]{1,0:T(8,128)(2,1)S(1)} %reshape.437), channel_id=1, replica_groups=mesh['wide'=32,'narrow'=16] {'narrow'}, dimensions={0}, use_global_device_ids=true | all-gather | bytes 417792 | tf_op jit(solution)/shard_map/all_gather | solution.py:191
  158.6 4.9 %collective-permute-start.10 = (s32[32,8]{0,1:T(8,128)S(1)}, s32[32,8]{0,1:T(8,128)S(1)}, u32[]{:S(2)}, u32[]{:S(2)}) collective-permute-start(s32[32,8]{0,1:T(8,128)S(1)} %pad_add_fusion.3), channel_id=1, source_target_pairs={{0,32},{32,0},{16,48},{48,16},{64,96},{96,64},{80,112},{112,80},{1... | collective-permute-start | bytes 3080 | tf_op jit(solution)/shard_map/ppermute | solution.py:25
  173.9 4.5 %collective-permute-start.12 = (s32[128,8]{0,1:T(8,128)S(1)}, s32[128,8]{0,1:T(8,128)S(1)}, u32[]{:S(2)}, u32[]{:S(2)}) collective-permute-start(s32[128,8]{0,1:T(8,128)S(1)} %pad_add_fusion.5), channel_id=1, source_target_pairs={{0,128},{128,0},{16,144},{144,16},{32,160},{160,32},{48,176},{176,... | collective-permute-start | bytes 12296 | tf_op jit(solution)/shard_map/ppermute | solution.py:25
  180.4 7.7 %collective-permute-start.13 = (s32[256,8]{0,1:T(8,128)S(1)}, s32[256,8]{0,1:T(8,128)S(1)}, u32[]{:S(2)}, u32[]{:S(2)}) collective-permute-start(s32[256,8]{0,1:T(8,128)S(1)} %pad_add_fusion.1), channel_id=1, source_target_pairs={{0,256},{256,0},{16,272},{272,16},{32,288},{288,32},{48,304},{304,... | collective-permute-start | bytes 24584 | tf_op jit(solution)/shard_map/ppermute | solution.py:25
  191.8 4.0 collective-permute-start.15
  208.5 4.7 %collective-permute-start.17 = (bf16[128,768]{1,0:T(8,128)(2,1)}, bf16[128,768]{1,0:T(8,128)(2,1)}, u32[]{:S(2)}, u32[]{:S(2)}) collective-permute-start(bf16[128,768]{1,0:T(8,128)(2,1)} %pad_maximum_fusion.6), channel_id=1, source_target_pairs={{0,128},{128,0},{16,144},{144,16},{32,160},{160,32},{48,176},{176,... | collective-permute-start | bytes 589832 | tf_op jit(solution)/shard_map/ppermute | solution.py:25
  229.9 4.1 collective-permute-start.7
  253.0 6.0 %collective-permute-start.18 = (bf16[256,768]{1,0:T(8,128)(2,1)S(1)}, bf16[256,768]{1,0:T(8,128)(2,1)}, u32[]{:S(2)}, u32[]{:S(2)}) collective-permute-start(bf16[256,768]{1,0:T(8,128)(2,1)S(1)} %pad_maximum_fusion.4), channel_id=1, source_target_pairs={{0,256},{256,0},{16,272},{272,16},{32,288},{288,32},{48,304},{304,... | collective-permute-start | bytes 1179656 | tf_op jit(solution)/shard_map/ppermute | solution.py:25
  265.3 7.9 %collective-permute-done.18 = bf16[256,768]{1,0:T(8,128)(2,1)} collective-permute-done((bf16[256,768]{1,0:T(8,128)(2,1)S(1)}, bf16[256,768]{1,0:T(8,128)(2,1)}, u32[]{:S(2)}, u32[]{:S(2)}) %collective-permute-start.18) | collective-permute-done | bytes 393248 | tf_op jit(solution)/shard_map/ppermute | solution.py:25
  278.3 7.0 %collective-permute-start.19 = (f32[256,12]{0,1:T(8,128)S(1)}, f32[256,12]{0,1:T(8,128)S(1)}, u32[]{:S(2)}, u32[]{:S(2)}) collective-permute-start(f32[256,12]{0,1:T(8,128)S(1)} %slice_select_fusion.9), channel_id=1, source_target_pairs={{0,256},{256,0},{16,272},{272,16},{32,288},{288,32},{48,304},{304,... | collective-permute-start | bytes 36872 | tf_op jit(solution)/shard_map/ppermute | solution.py:25
  291.8 5.9 %collective-permute-done.35 = f32[256,12]{0,1:T(8,128)S(1)} collective-permute-done((f32[256,12]{0,1:T(8,128)S(1)}, f32[256,12]{0,1:T(8,128)S(1)}, u32[]{:S(2)}, u32[]{:S(2)}) %collective-permute-start.35) | collective-permute-done | bytes 12320 | tf_op jit(solution)/shard_map/ppermute | solution.py:25
  300.3 4.8 %collective-permute-start.36 = (f32[128,12]{0,1:T(8,128)S(1)}, f32[128,12]{0,1:T(8,128)S(1)}, u32[]{:S(2)}, u32[]{:S(2)}) collective-permute-start(f32[128,12]{0,1:T(8,128)S(1)} %slice_select_fusion.14), channel_id=1, source_target_pairs={{0,128},{128,0},{16,144},{144,16},{32,160},{160,32},{48,176},{176,... | collective-permute-start | bytes 18440 | tf_op jit(solution)/shard_map/ppermute | solution.py:25
  317.3 4.0 collective-permute-start.22
  325.7 4.3 %collective-permute-start.27 = (f32[256,768]{0,1:T(8,128)}, f32[256,768]{0,1:T(8,128)}, u32[]{:S(2)}, u32[]{:S(2)}) collective-permute-start(f32[256,768]{0,1:T(8,128)} %bitcast.67), channel_id=1, source_target_pairs={{0,256},{256,0},{16,272},{272,16},{32,288},{288,32},{48,304},{304,... | collective-permute-start | bytes 2359304 | tf_op jit(solution)/shard_map/ppermute | solution.py:25
  352.8 10.9 %collective-permute-start.28 = (f32[128,768]{0,1:T(8,128)}, f32[128,768]{0,1:T(8,128)S(1)}, u32[]{:S(2)}, u32[]{:S(2)}) collective-permute-start(f32[128,768]{0,1:T(8,128)} %bitcast.69), channel_id=1, source_target_pairs={{0,128},{128,0},{16,144},{144,16},{32,160},{160,32},{48,176},{176,... | collective-permute-start | bytes 1179656 | tf_op jit(solution)/shard_map/ppermute | solution.py:25
  373.6 3.9 collective-permute-start.29
  378.7 4.5 %collective-permute-done.29 = f32[64,768]{0,1:T(8,128)S(1)} collective-permute-done((f32[64,768]{0,1:T(8,128)S(1)}, f32[64,768]{0,1:T(8,128)S(1)}, u32[]{:S(2)}, u32[]{:S(2)}) %collective-permute-start.29) | collective-permute-done | bytes 196640 | tf_op jit(solution)/shard_map/ppermute | solution.py:25
  389.2 9.7 %collective-permute-done.30 = f32[32,768]{0,1:T(8,128)S(1)} collective-permute-done((f32[32,768]{0,1:T(8,128)S(1)}, f32[32,768]{0,1:T(8,128)S(1)}, u32[]{:S(2)}, u32[]{:S(2)}) %collective-permute-start.30) | collective-permute-done | bytes 98336 | tf_op jit(solution)/shard_map/ppermute | solution.py:25
  405.5 4.6 %collective-permute-done.31 = f32[16,768]{0,1:T(8,128)} collective-permute-done((f32[16,768]{0,1:T(8,128)}, f32[16,768]{0,1:T(8,128)}, u32[]{:S(2)}, u32[]{:S(2)}) %collective-permute-start.31) | collective-permute-done | bytes 49184 | tf_op jit(solution)/shard_map/ppermute | solution.py:25
  (372 shorter events, 205.3 us)
Async XLA Ops:
  3.1 192.7 %collective-permute-start.3 = (bf16[32,768]{1,0:T(8,128)(2,1)}, bf16[32,768]{1,0:T(8,128)(2,1)}, u32[]{:S(2)}, u32[]{:S(2)}) collective-permute-start(bf16[32,768]{1,0:T(8,128)(2,1)} %reshape.412), channel_id=1, source_target_pairs={{0,16},{16,0},{32,48},{48,32},{64,80},{80,64},{96,112},{112,96},{1... | collective-permute-start | bytes 147464 | tf_op jit(solution)/shard_map/ppermute | solution.py:25
  7.3 156.2 %collective-permute-start = (s32[32,4]{0,1:T(4,128)}, s32[32,4]{0,1:T(4,128)}, u32[]{:S(2)}, u32[]{:S(2)}) collective-permute-start(s32[32,4]{0,1:T(4,128)} %copy.192), channel_id=1, source_target_pairs={{0,16},{16,0},{32,48},{48,32},{64,80},{80,64},{96,112},{112,96},{1... | collective-permute-start | bytes 1544 | tf_op jit(solution)/shard_map/ppermute | solution.py:25
  11.7 179.3 %collective-permute-start.14 = (bf16[16,768]{1,0:T(8,128)(2,1)}, bf16[16,768]{1,0:T(8,128)(2,1)}, u32[]{:S(2)}, u32[]{:S(2)}) collective-permute-start(bf16[16,768]{1,0:T(8,128)(2,1)} %reshape.420), channel_id=1, source_target_pairs={{0,16},{16,0},{32,48},{48,32},{64,80},{80,64},{96,112},{112,96},{1... | collective-permute-start | bytes 73736 | tf_op jit(solution)/shard_map/ppermute | solution.py:25
  15.9 142.0 %collective-permute-start.9 = (s32[16,8]{0,1:T(8,128)}, s32[16,8]{0,1:T(8,128)}, u32[]{:S(2)}, u32[]{:S(2)}) collective-permute-start(s32[16,8]{0,1:T(8,128)} %copy.205), channel_id=1, source_target_pairs={{0,16},{16,0},{32,48},{48,32},{64,80},{80,64},{96,112},{112,96},{1... | collective-permute-start | bytes 1544 | tf_op jit(solution)/shard_map/ppermute | solution.py:25
  158.6 8.1 %collective-permute-start.10 = (s32[32,8]{0,1:T(8,128)S(1)}, s32[32,8]{0,1:T(8,128)S(1)}, u32[]{:S(2)}, u32[]{:S(2)}) collective-permute-start(s32[32,8]{0,1:T(8,128)S(1)} %pad_add_fusion.3), channel_id=1, source_target_pairs={{0,32},{32,0},{16,48},{48,16},{64,96},{96,64},{80,112},{112,80},{1... | collective-permute-start | bytes 3080 | tf_op jit(solution)/shard_map/ppermute | solution.py:25
  180.4 9.4 %collective-permute-start.13 = (s32[256,8]{0,1:T(8,128)S(1)}, s32[256,8]{0,1:T(8,128)S(1)}, u32[]{:S(2)}, u32[]{:S(2)}) collective-permute-start(s32[256,8]{0,1:T(8,128)S(1)} %pad_add_fusion.1), channel_id=1, source_target_pairs={{0,256},{256,0},{16,272},{272,16},{32,288},{288,32},{48,304},{304,... | collective-permute-start | bytes 24584 | tf_op jit(solution)/shard_map/ppermute | solution.py:25
  191.8 8.2 %collective-permute-start.15 = (bf16[32,768]{1,0:T(8,128)(2,1)S(1)}, bf16[32,768]{1,0:T(8,128)(2,1)S(1)}, u32[]{:S(2)}, u32[]{:S(2)}) collective-permute-start(bf16[32,768]{1,0:T(8,128)(2,1)S(1)} %pad_maximum_fusion.9), channel_id=1, source_target_pairs={{0,32},{32,0},{16,48},{48,16},{64,96},{96,64},{80,112},{112,80},{1... | collective-permute-start | bytes 147464 | tf_op jit(solution)/shard_map/ppermute | solution.py:25
  204.8 9.4 %collective-permute-start.5 = (bf16[128,768]{1,0:T(8,128)(2,1)S(1)}, bf16[128,768]{1,0:T(8,128)(2,1)S(1)}, u32[]{:S(2)}, u32[]{:S(2)}) collective-permute-start(bf16[128,768]{1,0:T(8,128)(2,1)S(1)} %pad_maximum_fusion.5), channel_id=1, source_target_pairs={{0,64},{64,0},{16,80},{80,16},{32,96},{96,32},{48,112},{112,48},{1... | collective-permute-start | bytes 589832 | tf_op jit(solution)/shard_map/ppermute | solution.py:25
  208.5 43.4 %collective-permute-start.17 = (bf16[128,768]{1,0:T(8,128)(2,1)}, bf16[128,768]{1,0:T(8,128)(2,1)}, u32[]{:S(2)}, u32[]{:S(2)}) collective-permute-start(bf16[128,768]{1,0:T(8,128)(2,1)} %pad_maximum_fusion.6), channel_id=1, source_target_pairs={{0,128},{128,0},{16,144},{144,16},{32,160},{160,32},{48,176},{176,... | collective-permute-start | bytes 589832 | tf_op jit(solution)/shard_map/ppermute | solution.py:25
  241.9 9.4 %collective-permute-start.8 = (f32[32,12]{0,1:T(8,128)S(1)}, f32[32,12]{0,1:T(8,128)S(1)}, u32[]{:S(2)}, u32[]{:S(2)}) collective-permute-start(f32[32,12]{0,1:T(8,128)S(1)} %slice_select_fusion.26), channel_id=1, source_target_pairs={{0,16},{16,0},{32,48},{48,32},{64,80},{80,64},{96,112},{112,96},{1... | collective-permute-start | bytes 4616 | tf_op jit(solution)/shard_map/ppermute | solution.py:25
  248.6 16.0 %collective-permute-start.24 = (f32[128,768]{0,1:T(8,128)}, f32[128,768]{0,1:T(8,128)S(1)}, u32[]{:S(2)}, u32[]{:S(2)}) collective-permute-start(f32[128,768]{0,1:T(8,128)} %bitcast.54), channel_id=1, source_target_pairs={{0,64},{64,0},{16,80},{80,16},{32,96},{96,32},{48,112},{112,48},{1... | collective-permute-start | bytes 1179656 | tf_op jit(solution)/shard_map/ppermute | solution.py:25
  253.0 20.3 %collective-permute-start.18 = (bf16[256,768]{1,0:T(8,128)(2,1)S(1)}, bf16[256,768]{1,0:T(8,128)(2,1)}, u32[]{:S(2)}, u32[]{:S(2)}) collective-permute-start(bf16[256,768]{1,0:T(8,128)(2,1)S(1)} %pad_maximum_fusion.4), channel_id=1, source_target_pairs={{0,256},{256,0},{16,272},{272,16},{32,288},{288,32},{48,304},{304,... | collective-permute-start | bytes 1179656 | tf_op jit(solution)/shard_map/ppermute | solution.py:25
  278.3 13.5 %collective-permute-start.19 = (f32[256,12]{0,1:T(8,128)S(1)}, f32[256,12]{0,1:T(8,128)S(1)}, u32[]{:S(2)}, u32[]{:S(2)}) collective-permute-start(f32[256,12]{0,1:T(8,128)S(1)} %slice_select_fusion.9), channel_id=1, source_target_pairs={{0,256},{256,0},{16,272},{272,16},{32,288},{288,32},{48,304},{304,... | collective-permute-start | bytes 36872 | tf_op jit(solution)/shard_map/ppermute | solution.py:25
  288.2 9.5 %collective-permute-start.35 = (f32[256,12]{0,1:T(8,128)S(1)}, f32[256,12]{0,1:T(8,128)S(1)}, u32[]{:S(2)}, u32[]{:S(2)}) collective-permute-start(f32[256,12]{0,1:T(8,128)S(1)} %slice_select_fusion.8), channel_id=1, source_target_pairs={{0,256},{256,0},{16,272},{272,16},{32,288},{288,32},{48,304},{304,... | collective-permute-start | bytes 36872 | tf_op jit(solution)/shard_map/ppermute | solution.py:25
  317.3 12.7 %collective-permute-start.22 = (f32[32,12]{0,1:T(8,128)S(1)}, f32[32,12]{0,1:T(8,128)S(1)}, u32[]{:S(2)}, u32[]{:S(2)}) collective-permute-start(f32[32,12]{0,1:T(8,128)S(1)} %slice_select_fusion.20), channel_id=1, source_target_pairs={{0,32},{32,0},{16,48},{48,16},{64,96},{96,64},{80,112},{112,80},{1... | collective-permute-start | bytes 4616 | tf_op jit(solution)/shard_map/ppermute | solution.py:25
  321.4 8.6 %collective-permute-start.38 = (f32[32,12]{0,1:T(8,128)S(1)}, f32[32,12]{0,1:T(8,128)S(1)}, u32[]{:S(2)}, u32[]{:S(2)}) collective-permute-start(f32[32,12]{0,1:T(8,128)S(1)} %slice_select_fusion.12), channel_id=1, source_target_pairs={{0,32},{32,0},{16,48},{48,16},{64,96},{96,64},{80,112},{112,80},{1... | collective-permute-start | bytes 4616 | tf_op jit(solution)/shard_map/ppermute | solution.py:25
  325.7 23.9 %collective-permute-start.27 = (f32[256,768]{0,1:T(8,128)}, f32[256,768]{0,1:T(8,128)}, u32[]{:S(2)}, u32[]{:S(2)}) collective-permute-start(f32[256,768]{0,1:T(8,128)} %bitcast.67), channel_id=1, source_target_pairs={{0,256},{256,0},{16,272},{272,16},{32,288},{288,32},{48,304},{304,... | collective-permute-start | bytes 2359304 | tf_op jit(solution)/shard_map/ppermute | solution.py:25
  330.8 10.8 %collective-permute-start.23 = (f32[16,12]{0,1:T(8,128)S(1)}, f32[16,12]{0,1:T(8,128)S(1)}, u32[]{:S(2)}, u32[]{:S(2)}) collective-permute-start(f32[16,12]{0,1:T(8,128)S(1)} %slice_select_fusion.18), channel_id=1, source_target_pairs={{0,16},{16,0},{32,48},{48,32},{64,80},{80,64},{96,112},{112,96},{1... | collective-permute-start | bytes 2312 | tf_op jit(solution)/shard_map/ppermute | solution.py:25
  337.6 39.9 %collective-permute-start.25 = (f32[64,768]{0,1:T(8,128)}, f32[64,768]{0,1:T(8,128)}, u32[]{:S(2)}, u32[]{:S(2)}) collective-permute-start(f32[64,768]{0,1:T(8,128)} %bitcast.56), channel_id=1, source_target_pairs={{0,32},{32,0},{16,48},{48,16},{64,96},{96,64},{80,112},{112,80},{1... | collective-permute-start | bytes 589832 | tf_op jit(solution)/shard_map/ppermute | solution.py:25
  352.8 20.5 %collective-permute-start.28 = (f32[128,768]{0,1:T(8,128)}, f32[128,768]{0,1:T(8,128)S(1)}, u32[]{:S(2)}, u32[]{:S(2)}) collective-permute-start(f32[128,768]{0,1:T(8,128)} %bitcast.69), channel_id=1, source_target_pairs={{0,128},{128,0},{16,144},{144,16},{32,160},{160,32},{48,176},{176,... | collective-permute-start | bytes 1179656 | tf_op jit(solution)/shard_map/ppermute | solution.py:25
  373.6 9.7 %collective-permute-start.29 = (f32[64,768]{0,1:T(8,128)S(1)}, f32[64,768]{0,1:T(8,128)S(1)}, u32[]{:S(2)}, u32[]{:S(2)}) collective-permute-start(f32[64,768]{0,1:T(8,128)S(1)} %bitcast.187), channel_id=1, source_target_pairs={{0,64},{64,0},{16,80},{80,16},{32,96},{96,32},{48,112},{112,48},{1... | collective-permute-start | bytes 589832 | tf_op jit(solution)/shard_map/ppermute | solution.py:25
  383.6 15.3 %collective-permute-start.30 = (f32[32,768]{0,1:T(8,128)S(1)}, f32[32,768]{0,1:T(8,128)S(1)}, u32[]{:S(2)}, u32[]{:S(2)}) collective-permute-start(f32[32,768]{0,1:T(8,128)S(1)} %bitcast.188), channel_id=1, source_target_pairs={{0,32},{32,0},{16,48},{48,16},{64,96},{96,64},{80,112},{112,80},{1... | collective-permute-start | bytes 294920 | tf_op jit(solution)/shard_map/ppermute | solution.py:25
  386.6 15.8 %collective-permute-start.26 = (f32[32,768]{0,1:T(8,128)S(1)}, f32[32,768]{0,1:T(8,128)S(1)}, u32[]{:S(2)}, u32[]{:S(2)}) collective-permute-start(f32[32,768]{0,1:T(8,128)S(1)} %bitcast.185), channel_id=1, source_target_pairs={{0,16},{16,0},{32,48},{48,32},{64,80},{80,64},{96,112},{112,96},{1... | collective-permute-start | bytes 294920 | tf_op jit(solution)/shard_map/ppermute | solution.py:25
  400.0 10.0 %collective-permute-start.31 = (f32[16,768]{0,1:T(8,128)}, f32[16,768]{0,1:T(8,128)}, u32[]{:S(2)}, u32[]{:S(2)}) collective-permute-start(f32[16,768]{0,1:T(8,128)} %bitcast.75), channel_id=1, source_target_pairs={{0,16},{16,0},{32,48},{48,32},{64,80},{80,64},{96,112},{112,96},{1... | collective-permute-start | bytes 147464 | tf_op jit(solution)/shard_map/ppermute | solution.py:25
  (68 other events, 1138.6 us)
where the time goes:
time: 418 us; the launch traced here: 415 us
  starting transfers between devices  148 us (35%)
  blocking collectives  105 us (25%)
  waiting for transfers between devices  58 us (14%)
  local copies, waits for them, and re-layouts  48.6 us (12%)
  other arithmetic  30.8 us (7%)
  matrix products  23.5 us (6%)
    ppermute x40, starting transfers between devices, from_partner(): return lax.ppermute(block, axis, route)  148 us
    ppermute x40, waiting for transfers between devices, from_partner(): return lax.ppermute(block, axis, route)  58 us
    all_gather x1, blocking collectives, local(): lax.all_gather(near_ids, 'narrow', axis=0, tiled=True)  23.2 us
    all_gather x1, blocking collectives, local(): lax.all_gather(pick(values, RATE_NEAR).reshape(near_count, width), 'narro...  17.9 us
    all_gather x1, blocking collectives, local(): lax.all_gather(pick(keys, RATE_NEAR).reshape(near_count, width), 'narrow'...  16.9 us
    all_gather x1, blocking collectives, local(): lax.all_gather(pick(keys, RATE_FAR).reshape(far_count, width), 'narrow',...  16.8 us
    all_gather x1, blocking collectives, local(): lax.all_gather(pick(values, RATE_FAR).reshape(far_count, width), 'narrow'...  15.6 us
    all_gather x1, blocking collectives, local(): lax.all_gather(slide_ids.reshape(far_count, RATE_FAR), 'narrow', axis=0,...  14.7 us
  transfers between devices with their start and end apart: 40, of which 18 were waited for; matrix products, arithmetic and copies ran while one was open for 21% of the time, Pallas kernels for 0%

commit v1 on v0

v1 whole, which is shorter than its diff:
```python
import jax
import jax.numpy as jnp
from jax import lax
from jax.experimental import pallas as pl
from jax.experimental.pallas import tpu as pltpu
from jax.sharding import PartitionSpec as P

MESH = pl.DeviceIdType.MESH
HEADS = 12
HDIM = 64
WIDTH = 768
TOK = 128
WIDE = 32
SEG = 8
REACH = 6
PARTNERS = 2 * REACH
PENALTY = 2048.0
ABSENT = -1e30
BF16 = jnp.bfloat16
F32 = jnp.float32

KV_PARTS = ((0, 5), (5, 4), (9, 4))


def lanes_of(shape):
    return lax.broadcasted_iota(jnp.int32, shape, len(shape) - 1)


def nt_dot(left, right):
    return lax.dot_general(left, right, (((1,), (1,)), ((), ())), preferred_element_type=F32)


def nn_dot(left, right):
    return lax.dot_general(left, right, (((1,), (0,)), ((), ())), preferred_element_type=F32)


def out_slot(sender_at, receiver_at):
    return lax.rem(sender_at - receiver_at + 15, 8) - (receiver_at < 7).astype(jnp.int32)


def kernel(
    q_ref, k_ref, v_ref, ids_ref, w_hbm, out_ref,
    pq, pk, pv, pc, kv_sel, q_sel, kv, kv_roll, q_in, q_out, q_roll, o_in, o_out, r_in, r_out,
    stat_in, stat_out, loc_o, loc_l, att, w_vmem,
    w_sem, pair_send, pair_recv, ring_send, ring_recv,
    q_send, q_recv_in, q_recv_out, o_send, o_recv_in, o_recv_out,
):
    g = lax.axis_index("wide")
    n = lax.axis_index("narrow")
    place = lax.rem(g, SEG)
    core = lax.rem(n, 2)
    pair = (g, n + 1 - 2 * core)
    right = (g, lax.rem(n + 2, 16))
    left = (g, lax.rem(n + 14, 16))

    def partner(i):
        offset = i - REACH + (i >= REACH).astype(jnp.int32)
        other = lax.rem(g + offset + WIDE, WIDE)
        return other, lax.rem(other, SEG), other // SEG == g // SEG

    empty = jnp.where(lax.rem(lanes_of((2, 16, 128)), 8) == 0, ABSENT, 0.0).astype(BF16)
    spare = SEG - 1 - place
    r_in[spare] = jnp.zeros((2, 7, 16, 128), BF16)
    r_in[spare, :, 0] = empty
    r_out[5] = jnp.zeros((2, 4, 16, 128), BF16)
    r_out[5, :, 0] = empty

    w_copy = pltpu.make_async_copy(w_hbm, w_vmem, w_sem)
    w_copy.start()

    barrier = pltpu.get_barrier_semaphore()
    for device in (pair, right, left):
        pl.semaphore_signal(barrier, inc=1, device_id=device, device_id_type=MESH)

    @pl.loop(0, PARTNERS)
    def _(i):
        other, _, _ = partner(i)
        for side in range(2):
            pl.semaphore_signal(
                barrier, inc=1, device_id=(other, n - core + side), device_id_type=MESH
            )

    row = lax.broadcasted_iota(jnp.int32, (TOK, TOK), 0)
    col = lax.broadcasted_iota(jnp.int32, (TOK, TOK), 1)
    order = (col == 8 * (row % 16) + row // 16).astype(F32).astype(BF16)
    unlike = (jnp.broadcast_to(ids_ref[...], (TOK, TOK)) != row % 16).astype(F32).astype(BF16)
    sorted_c = nt_dot(order, unlike)
    pc[...] = sorted_c.astype(BF16)
    lane16 = lanes_of((16, 128))
    low16 = lane16 < HDIM
    others = jnp.zeros((16, 128), F32)
    for residue in range(8):
        others = jnp.where(
            lane16 // 16 == residue, sorted_c[residue * 16:residue * 16 + 16], others
        )
    others = others.astype(BF16)
    for half in range(2):
        kv_sel[half, 0] = others
        q_sel[half, 0] = others

    def picked(source, a, shift):
        first = (2 * a + shift) % 8
        block = source[:, a * 128:(a + 1) * 128]
        return jnp.where(
            low16, block[first * 16:first * 16 + 16], block[first * 16 + 16:first * 16 + 32]
        ).astype(BF16)

    sorted_k = nn_dot(order, k_ref[...])
    pk[...] = sorted_k.astype(BF16)
    for a in range(6):
        for part in range(2):
            kv_sel[a // 3, 1 + 4 * (a % 3) + part] = picked(sorted_k, a, 4 * part)
    sorted_v = nn_dot(order, v_ref[...])
    pv[...] = sorted_v.astype(BF16)
    for a in range(6):
        for part in range(2):
            kv_sel[a // 3, 3 + 4 * (a % 3) + part] = picked(sorted_v, a, 4 * part)
    kv[core] = kv_sel[core]
    sorted_q = nn_dot(order, q_ref[...]) * (HDIM ** -0.5)
    pq[...] = sorted_q.astype(BF16)
    for a in range(6):
        for part in range(2):
            q_sel[a // 3, 1 + 3 * part + a % 3] = picked(sorted_q, a, 4 * part)
    q_in[place, core] = q_sel[core]

    pl.semaphore_wait(barrier, 3 + 2 * PARTNERS)

    pair_kv = pltpu.make_async_remote_copy(
        kv_sel.at[1 - core], kv.at[core], pair_send.at[0], pair_recv.at[0],
        device_id=pair, device_id_type=MESH,
    )
    pair_kv.start()
    pair_q = pltpu.make_async_remote_copy(
        q_sel.at[1 - core], q_in.at[place, core], pair_send.at[1], pair_recv.at[1],
        device_id=pair, device_id_type=MESH,
    )
    pair_q.start()

    def ring_copy(step, way, part):
        source = step if way == 0 else (8 - step) % 8
        target = source + 1 if way == 0 else (source + 7) % 8
        first, count = KV_PARTS[part]
        if step < 3:
            at, to, rows, arrived = 2 * source, 2 * target, 2, target
        else:
            at, to, rows, arrived = 2 * source + way, 2 * target + way, 1, 4 * (1 - way)
        return pltpu.make_async_remote_copy(
            kv.at[pl.ds(at, rows), pl.ds(first, count)],
            kv.at[pl.ds(to, rows), pl.ds(first, count)],
            ring_send.at[(step * 2 + way) * 3 + part],
            ring_recv.at[arrived * 3 + part],
            device_id=right if way == 0 else left, device_id_type=MESH,
        )

    def ring_step(step):
        for part in range(3):
            for way in range(2):
                if step > 0:
                    ring_copy(step - 1, way, part).wait_recv()
                if step < 4:
                    ring_copy(step, way, part).start()

    pair_kv.wait_recv()
    ring_step(0)

    def q_copy(i, side, inside):
        other, other_at, _ = partner(i)
        if inside:
            source, target, arrived = q_sel.at[side], q_in.at[place, core], q_recv_in.at[place, core]
        else:
            slot = out_slot(place, other_at)
            source, target = q_sel.at[side, pl.ds(0, 4)], q_out.at[slot, core]
            arrived = q_recv_out.at[slot, core]
        return pltpu.make_async_remote_copy(
            source, target, q_send.at[2 * i + side], arrived,
            device_id=(other, n - core + side), device_id_type=MESH,
        )

    def for_partners(act):
        @pl.loop(0, PARTNERS)
        def _(i):
            _, _, same = partner(i)

            @pl.when(same)
            def _():
                for side in range(2):
                    act(i, side, True)

            @pl.when(jnp.logical_not(same))
            def _():
                for side in range(2):
                    act(i, side, False)

    for_partners(lambda i, side, inside: q_copy(i, side, inside).start())

    ones = jnp.ones((TOK, 128), BF16)
    lane128 = lanes_of((TOK, 128))
    own_slide = jnp.where(lane128 < 16, (sorted_c - 1.0) * PENALTY, 0.0).astype(BF16)
    wide_low = lanes_of((TOK, 128)) < HDIM

    def local_pair(a):
        cols = slice(a * 128, (a + 1) * 128)
        block = pq[:, cols].astype(F32)
        left_side = jnp.concatenate(
            [
                jnp.concatenate([jnp.where(wide_low, block, 0.0).astype(BF16), own_slide], 1),
                jnp.concatenate([jnp.where(wide_low, 0.0, block).astype(BF16), own_slide], 1),
            ],
            0,
        )
        scores = nt_dot(left_side, jnp.concatenate([pk[:, cols], pc[...]], 1))
        top = jnp.max(scores, axis=1, keepdims=True)
        weights = jnp.exp(scores - top).astype(BF16)
        summed = nn_dot(weights, jnp.concatenate([pv[:, cols], ones], 1))
        result = summed[:, :128] / summed[:, 128:]
        level = top + jnp.log(summed[:, 128:])
        loc_o[:, cols] = jnp.where(wide_low, result[:TOK], result[TOK:])
        loc_l[:, cols] = jnp.where(wide_low, level[:TOK], level[TOK:])

    local_pair(0)
    local_pair(1)
    ring_step(1)
    local_pair(2)
    local_pair(3)
    ring_step(2)
    local_pair(4)
    local_pair(5)
    ring_step(3)

    pair_q.wait_recv()

    @pl.loop(0, PARTNERS)
    def _(i):
        other, other_at, same = partner(i)

        @pl.when(same)
        def _():
            for side in range(2):
                spot = q_in.at[other_at, side]
                pltpu.make_async_copy(spot, spot, q_recv_in.at[other_at, side]).wait()

        @pl.when(jnp.logical_not(same))
        def _():
            slot = out_slot(other_at, place)
            for side in range(2):
                spot = q_out.at[slot, side]
                pltpu.make_async_copy(spot, spot, q_recv_out.at[slot, side]).wait()

    for side in range(2):
        for slot in range(SEG):
            q_roll[slot, side] = pltpu.roll(q_in[slot, side, 0].astype(F32), 64, 1).astype(BF16)
    ring_step(4)
    for slot in range(16):
        kv_roll[slot] = pltpu.roll(kv[slot, 0].astype(F32), 64, 1).astype(BF16)

    stat_in[...] = jnp.zeros(stat_in.shape, F32)
    stat_out[...] = jnp.zeros(stat_out.shape, F32)
    many = jnp.ones((256, 128), BF16)
    half_masks = [
        jnp.where(low16, 1.0, 0.0).astype(BF16), jnp.where(low16, 0.0, 1.0).astype(BF16)
    ]

    def stacked(ref_value):
        return ref_value.reshape(-1, 128)

    def blocks(a, total, first, rows):
        low = lanes_of((rows, 128)) < HDIM
        return jnp.where(low, a[first:first + rows], a[total + first:total + first + rows])

    def group_pair(j):
        masks = []
        for u in range(2):
            residue = lax.rem(6 * core + 2 * j + u, 8)
            masks.append(jnp.where(lane16 // 16 == residue, PENALTY, 0.0).astype(BF16))
        near_c = stacked(kv[:, 0])
        turned_c = stacked(kv_roll[...])
        far_k = jnp.concatenate([stacked(kv[:, 1 + 4 * j]), near_c], 1)
        near_k = jnp.concatenate([stacked(kv[:, 2 + 4 * j]), turned_c], 1)
        far_v = jnp.concatenate([stacked(kv[:, 3 + 4 * j]), many], 1)
        near_v = jnp.concatenate([stacked(kv[:, 4 + 4 * j]), many], 1)

        def left_side(block, slides, u):
            return jnp.concatenate(
                [stacked(block * half_masks[u]), stacked((slides - 1) * masks[u])], 1
            )

        def levels(top, totals):
            return jnp.where(top < -PENALTY / 2, ABSENT, top + jnp.log(totals))

        def inside(first, count):
            rows = count * 32
            far_q, near_q = q_in[first:first + count, :, 1 + j], q_in[first:first + count, :, 4 + j]
            slides, turned = q_in[first:first + count, :, 0], q_roll[first:first + count]
            lhs = jnp.concatenate(
                [
                    left_side(far_q, slides, 0), left_side(near_q, turned, 0),
                    left_side(far_q, slides, 1), left_side(near_q, turned, 1),
                ],
                0,
            )
            far_s, near_s = nt_dot(lhs, far_k), nt_dot(lhs, near_k)
            top = jnp.max(jnp.maximum(far_s, near_s), axis=1, keepdims=True)
            far_o = nn_dot(jnp.exp(far_s - top).astype(BF16), far_v)
            near_o = nn_dot(jnp.exp(near_s - top).astype(BF16), near_v)
            both = far_o + near_o
            for part in range(2):
                at = [part * rows, (2 + part) * rows]
                outs, lev = [], []
                for start in at:
                    total = both[start:start + rows]
                    if part == 0:
                        total = total + far_o[start:start + rows]
                    outs.append(total[:, :128] / total[:, 128:])
                    lev.append(levels(top[start:start + rows], total[:, 128:]))
                low = lanes_of((rows, 128)) < HDIM
                o_in[first:first + count, :, 1 + 3 * part + j] = (
                    jnp.where(low, outs[0], outs[1]).astype(BF16).reshape(count, 2, 16, 128)
                )
                spot = lanes_of((rows, 128)) // 8
                kept = stacked(stat_in[first:first + count])
                for u in range(2):
                    kept = jnp.where(spot == 8 * part + 2 * j + u, lev[u], kept)
                stat_in[first:first + count] = kept.reshape(count, 2, 16, 128)

        def outside(first, count):
            rows = count * 32
            far_q, slides = q_out[first:first + count, :, 1 + j], q_out[first:first + count, :, 0]
            lhs = jnp.concatenate([left_side(far_q, slides, 0), left_side(far_q, slides, 1)], 0)
            far_s = nt_dot(lhs, far_k)
            top = jnp.max(far_s, axis=1, keepdims=True)
            total = nn_dot(jnp.exp(far_s - top).astype(BF16), far_v)
            result = total[:, :128] / total[:, 128:]
            lev = levels(top, total[:, 128:])
            low = lanes_of((rows, 128)) < HDIM
            o_out[first:first + count, :, 1 + j] = (
                jnp.where(low, result[:rows], result[rows:]).astype(BF16).reshape(count, 2, 16, 128)
            )
            spot = lanes_of((rows, 128)) // 8
            kept = stacked(stat_out[first:first + count])
            for u in range(2):
                kept = jnp.where(spot == 2 * j + u, lev[u * rows:(u + 1) * rows], kept)
            stat_out[first:first + count] = kept.reshape(count, 2, 16, 128)

        for first in range(0, 8, 2):
            inside(first, 2)
        for first in range(0, 6, 3):
            outside(first, 3)

    @pl.loop(0, 3)
    def _(j):
        group_pair(j)

    def in_pieces(level):
        high = level.astype(BF16).astype(F32)
        rest = level - high
        middle = rest.astype(BF16).astype(F32)
        last = rest - middle
        at = lax.rem(lanes_of(level.shape), 8)
        pieces = jnp.where(
            at == 0, high, jnp.where(at == 1, middle, jnp.where(at == 2, last, 0.0))
        )
        return pieces.astype(BF16)

    o_in[:, :, 0] = in_pieces(stat_in[...])
    o_out[:, :, 0] = in_pieces(stat_out[...])

    def o_copy(i, side, inside):
        other, other_at, _ = partner(i)
        if inside:
            source, target, arrived = o_in.at[other_at, side], r_in.at[place, core], o_recv_in.at[place, core]
        else:
            slot = out_slot(place, other_at)
            source, target = o_out.at[out_slot(other_at, place), side], r_out.at[slot, core]
            arrived = o_recv_out.at[slot, core]
        return pltpu.make_async_remote_copy(
            source, target, o_send.at[2 * i + side], arrived,
            device_id=(other, n - core + side), device_id_type=MESH,
        )

    for_partners(lambda i, side, inside: o_copy(i, side, inside).start())
    pair_o = pltpu.make_async_remote_copy(
        o_in.at[place, 1 - core], r_in.at[place, core], pair_send.at[2], pair_recv.at[2],
        device_id=pair, device_id_type=MESH,
    )
    pair_o.start()
    r_in[place, core] = o_in[place, core]
    att[...] = loc_o[...]

    @pl.loop(0, PARTNERS)
    def _(i):
        other, other_at, same = partner(i)

        @pl.when(same)
        def _():
            for side in range(2):
                spot = r_in.at[other_at, side]
                pltpu.make_async_copy(spot, spot, o_recv_in.at[other_at, side]).wait()

        @pl.when(jnp.logical_not(same))
        def _():
            slot = out_slot(other_at, place)
            for side in range(2):
                spot = r_out.at[slot, side]
                pltpu.make_async_copy(spot, spot, o_recv_out.at[slot, side]).wait()

    pair_o.wait_recv()

    e_row = lax.broadcasted_iota(jnp.int32, (128, 384), 0)
    e_col = lax.broadcasted_iota(jnp.int32, (128, 384), 1)
    to_far = jnp.where((e_row // 8 == e_col // 64) & (e_row % 8 < 3), 1.0, 0.0).astype(BF16)
    to_near = jnp.where((e_row // 8 == e_col // 64 + 8) & (e_row % 8 < 3), 1.0, 0.0).astype(BF16)
    for half in range(2):
        stats_i = r_in[:, half, 0].reshape(128, 128)
        stats_o = r_out[:, half, 0].reshape(96, 128)
        far_i = nn_dot(stats_i, to_far)
        near_i = nn_dot(stats_i, to_near)
        far_o = nn_dot(stats_o, to_far)
        for j in range(3):
            a = 3 * half + j
            lanes = slice(j * 128, (j + 1) * 128)
            cols = slice(a * 128, (a + 1) * 128)
            for part in range(2):
                r0 = (2 * a + 4 * part) % 8 * 16
                r1 = r0 + 16
                own_l = jnp.where(low16, loc_l[r0:r0 + 16, cols], loc_l[r1:r1 + 16, cols])
                own_o = jnp.where(low16, loc_o[r0:r0 + 16, cols], loc_o[r1:r1 + 16, cols])
                lev = (near_i if part else far_i)[:, lanes].reshape(8, 16, 128)
                val = r_in[:, half, 1 + 3 * part + j].astype(F32)
                if part == 0:
                    lev = jnp.concatenate([lev, far_o[:, lanes].reshape(6, 16, 128)], 0)
                    val = jnp.concatenate([val, r_out[:, half, 1 + j].astype(F32)], 0)
                top = jnp.maximum(jnp.max(lev, axis=0), own_l)
                scale = jnp.exp(lev - top[None])
                own_scale = jnp.exp(own_l - top)
                numer = jnp.sum(scale * val, axis=0) + own_scale * own_o
                denom = jnp.sum(scale, axis=0) + own_scale
                joined = numer / denom
                att[r0:r0 + 16, a * 128:a * 128 + 64] = joined[:, :64]
                att[r1:r1 + 16, a * 128 + 64:a * 128 + 128] = joined[:, 64:]

    back = (row == 8 * (col % 16) + col // 16).astype(F32).astype(BF16)
    attended = nn_dot(back, att[...].astype(BF16)).astype(BF16)
    w_copy.wait()
    out_ref[...] = nn_dot(attended, w_vmem[...]).astype(BF16)

    pair_kv.wait_send()
    pair_q.wait_send()
    pair_o.wait_send()
    for step in range(4):
        for way in range(2):
            for part in range(3):
                ring_copy(step, way, part).wait_send()

    def sent(i, side, inside):
        q_copy(i, side, inside).wait_send()
        o_copy(i, side, inside).wait_send()

    for_partners(sent)


def local(queries, keys, values, slide_ids, w_out):
    vmem = pl.BlockSpec(memory_space=pltpu.VMEM)
    dma = pltpu.SemaphoreType.DMA
    return pl.pallas_call(
        kernel,
        out_shape=jax.ShapeDtypeStruct((TOK, WIDTH), BF16),
        in_specs=[vmem, vmem, vmem, vmem, pl.BlockSpec(memory_space=pl.ANY)],
        out_specs=vmem,
        scratch_shapes=[
            pltpu.VMEM((TOK, WIDTH), BF16),
            pltpu.VMEM((TOK, WIDTH), BF16),
            pltpu.VMEM((TOK, WIDTH), BF16),
            pltpu.VMEM((TOK, 128), BF16),
            pltpu.VMEM((2, 13, 16, 128), BF16),
            pltpu.VMEM((2, 7, 16, 128), BF16),
            pltpu.VMEM((16, 13, 16, 128), BF16),
            pltpu.VMEM((16, 16, 128), BF16),
            pltpu.VMEM((8, 2, 7, 16, 128), BF16),
            pltpu.VMEM((6, 2, 4, 16, 128), BF16),
            pltpu.VMEM((8, 2, 16, 128), BF16),
            pltpu.VMEM((8, 2, 7, 16, 128), BF16),
            pltpu.VMEM((6, 2, 4, 16, 128), BF16),
            pltpu.VMEM((8, 2, 7, 16, 128), BF16),
            pltpu.VMEM((6, 2, 4, 16, 128), BF16),
            pltpu.VMEM((8, 2, 16, 128), F32),
            pltpu.VMEM((6, 2, 16, 128), F32),
            pltpu.VMEM((TOK, WIDTH), F32),
            pltpu.VMEM((TOK, WIDTH), F32),
            pltpu.VMEM((TOK, WIDTH), F32),
            pltpu.VMEM((WIDTH, WIDTH), BF16),
            dma,
            dma((3,)),
            dma((3,)),
            dma((24,)),
            dma((24,)),
            dma((24,)),
            dma((8, 2)),
            dma((6, 2)),
            dma((24,)),
            dma((8, 2)),
            dma((6, 2)),
        ],
        compiler_params=pltpu.CompilerParams(
            collective_id=0, has_side_effects=True, vmem_limit_bytes=40 * 1024 * 1024
        ),
        name="dilated",
    )(queries, keys, values, slide_ids.reshape(1, TOK), w_out)


def solution(mesh):
    placed = (
        P(("wide", "narrow"), None),
        P(("wide", "narrow"), None),
        P(("wide", "narrow"), None),
        P(("wide", "narrow")),
        P(),
    )
    return jax.shard_map(
        local, mesh=mesh, in_specs=placed, out_specs=P(("wide", "narrow"), None), check_vma=False
    )
```

time: 418 us -> 53 us (0.13)
  the two profiles are of different devices: /device:TPU:8 before, /device:TPU:1 now
where the time goes in v1:
time: 53 us; the launch traced here: 52.8 us
  Pallas kernels  47.4 us (89%)
  local copies, waits for them, and re-layouts  5.38 us (10%)
    pallas_call x1, Pallas kernels, local(): pl.pallas_call(kernel, out_shape=jax.ShapeDtypeStruct((TOK, WIDTH), BF16)...  47.4 us
    unnamed x11, local copies, waits for them, and re-layouts  5.38 us

profile of v1, /device:TPU:1, one launch (start us, length us, event | category | flops | bytes accessed | tf_op | source)
XLA Modules:
  0.0 52.8 jit_solution(18176519007657141346)
XLA Ops:
  0.0 0.0 copy-start
  0.0 1.3 %copy-done = bf16[768,768]{1,0:T(8,128)(2,1)S(1)} copy-done((bf16[768,768]{1,0:T(8,128)(2,1)S(1)}, bf16[768,768]{1,0:T(8,128)(2,1)}, u32[]{:S(2)}) %copy-start) | copy-done | bytes 1179672
  1.3 0.0 copy-start.1
  1.3 0.9 %copy-done.1 = bf16[128,768]{1,0:T(8,128)(2,1)S(1)} copy-done((bf16[128,768]{1,0:T(8,128)(2,1)S(1)}, bf16[128,768]{1,0:T(8,128)(2,1)}, u32[]{:S(2)}) %copy-start.1) | copy-done | bytes 196632
  2.2 0.0 copy-start.2
  2.2 0.9 %copy-done.2 = bf16[128,768]{1,0:T(8,128)(2,1)S(1)} copy-done((bf16[128,768]{1,0:T(8,128)(2,1)S(1)}, bf16[128,768]{1,0:T(8,128)(2,1)}, u32[]{:S(2)}) %copy-start.2) | copy-done | bytes 196632
  3.1 0.0 copy-start.3
  3.1 0.9 %copy-done.3 = bf16[128,768]{1,0:T(8,128)(2,1)S(1)} copy-done((bf16[128,768]{1,0:T(8,128)(2,1)S(1)}, bf16[128,768]{1,0:T(8,128)(2,1)}, u32[]{:S(2)}) %copy-start.3) | copy-done | bytes 196632
  4.1 0.0 copy-start.4
  4.1 0.7 %copy-done.4 = s32[128]{0:T(128)S(1)} copy-done((s32[128]{0:T(128)S(1)}, s32[128]{0:T(128)}, u32[]{:S(2)}) %copy-start.4) | copy-done | bytes 536
  4.7 47.4 %dilated.1 = bf16[128,768]{1,0:T(8,128)(2,1)S(1)} custom-call(bf16[128,768]{1,0:T(8,128)(2,1)S(1)} %copy-done.1, bf16[128,768]{1,0:T(8,128)(2,1)S(1)} %copy-done.2, bf16[128,768]{1,0:T(8,128)(2,1)S(1)} %copy-done.3, s32[1,128]{1,0:T(1,128)S(1)} %bitcast.1, bf16[768,768]{1,0:T(8,128)(2,1)S(1)} %copy-done), custom_call_target="tpu_custom_call" | custom-call | tf_op jit(solution)/shard_map/dilated/pallas_call | solution.py:464
  52.1 0.7 %copy.7 = bf16[128,768]{1,0:T(8,128)(2,1)} copy(bf16[128,768]{1,0:T(8,128)(2,1)S(1)} %dilated.1) | data formatting | bytes 393216
Async XLA Ops:
  0.0 1.3 %copy-start = (bf16[768,768]{1,0:T(8,128)(2,1)S(1)}, bf16[768,768]{1,0:T(8,128)(2,1)}, u32[]{:S(2)}) copy-start(bf16[768,768]{1,0:T(8,128)(2,1)} %w_hbm.1) | copy-start | bytes 3538948
  1.3 0.9 %copy-start.1 = (bf16[128,768]{1,0:T(8,128)(2,1)S(1)}, bf16[128,768]{1,0:T(8,128)(2,1)}, u32[]{:S(2)}) copy-start(bf16[128,768]{1,0:T(8,128)(2,1)} %q_ref.1) | copy-start | bytes 589828
  2.2 0.9 %copy-start.2 = (bf16[128,768]{1,0:T(8,128)(2,1)S(1)}, bf16[128,768]{1,0:T(8,128)(2,1)}, u32[]{:S(2)}) copy-start(bf16[128,768]{1,0:T(8,128)(2,1)} %k_ref.1) | copy-start | bytes 589828
  3.1 0.9 %copy-start.3 = (bf16[128,768]{1,0:T(8,128)(2,1)S(1)}, bf16[128,768]{1,0:T(8,128)(2,1)}, u32[]{:S(2)}) copy-start(bf16[128,768]{1,0:T(8,128)(2,1)} %v_ref.1) | copy-start | bytes 589828
  4.1 0.7 %copy-start.4 = (s32[128]{0:T(128)S(1)}, s32[128]{0:T(128)}, u32[]{:S(2)}) copy-start(s32[128]{0:T(128)} %param.8) | copy-start | bytes 1540

commit v2 on v1

v2 whole, which is shorter than its diff:
```python
import jax
import jax.numpy as jnp
from jax import lax
from jax.experimental import pallas as pl
from jax.experimental.pallas import tpu as pltpu
from jax.sharding import PartitionSpec as P

MESH = pl.DeviceIdType.MESH
HEADS = 12
HDIM = 64
WIDTH = 768
TOK = 128
WIDE = 32
SEG = 8
REACH = 6
PARTNERS = 2 * REACH
PENALTY = 2048.0
ABSENT = -1e30
BF16 = jnp.bfloat16
F32 = jnp.float32

KV_PARTS = ((0, 5), (5, 4), (9, 4))


def lanes_of(shape):
    return lax.broadcasted_iota(jnp.int32, shape, len(shape) - 1)


def nt_dot(left, right):
    return lax.dot_general(left, right, (((1,), (1,)), ((), ())), preferred_element_type=F32)


def nn_dot(left, right):
    return lax.dot_general(left, right, (((1,), (0,)), ((), ())), preferred_element_type=F32)


def out_slot(sender_at, receiver_at):
    return lax.rem(sender_at - receiver_at + 15, 8) - (receiver_at < 7).astype(jnp.int32)


def kernel(
    q_hbm, k_hbm, v_hbm, ids_hbm, w_hbm, out_ref,
    q_ref, k_ref, v_ref, ids_ref,
    pq, pk, pv, pc, kv_sel, q_sel, kv, kv_roll, q_in, q_out, q_roll, o_in, o_out, r_in, r_out,
    loc_o, loc_l, att, w_vmem,
    in_sem, pair_send, pair_recv, ring_send, ring_recv,
    q_send, q_recv_in, q_recv_out, o_send_in, o_send_out, o_recv_in, o_recv_out,
):
    g = lax.axis_index("wide")
    n = lax.axis_index("narrow")
    place = lax.rem(g, SEG)
    core = lax.rem(n, 2)
    pair = (g, n + 1 - 2 * core)
    right = (g, lax.rem(n + 2, 16))
    left = (g, lax.rem(n + 14, 16))
    right2 = (g, lax.rem(n + 4, 16))
    left2 = (g, lax.rem(n + 12, 16))

    def partner(i):
        offset = i - REACH + (i >= REACH).astype(jnp.int32)
        other = lax.rem(g + offset + WIDE, WIDE)
        return other, lax.rem(other, SEG), other // SEG == g // SEG

    empty = jnp.where(lax.rem(lanes_of((2, 16, 128)), 8) == 0, ABSENT, 0.0).astype(BF16)
    spare = SEG - 1 - place
    r_in[spare] = jnp.zeros((2, 7, 16, 128), BF16)
    r_in[spare, :, 0] = empty
    r_out[5] = jnp.zeros((2, 4, 16, 128), BF16)
    r_out[5, :, 0] = empty

    loads = [
        pltpu.make_async_copy(source, target, in_sem.at[at])
        for at, (source, target) in enumerate(
            ((ids_hbm, ids_ref), (k_hbm, k_ref), (v_hbm, v_ref), (q_hbm, q_ref), (w_hbm, w_vmem))
        )
    ]
    for load in loads:
        load.start()

    barrier = pltpu.get_barrier_semaphore()
    turn = 1 - 2 * core
    crossed = ((g, right[1] + turn), (g, left[1] + turn))
    for device in (pair, right, left, right2, left2) + crossed:
        pl.semaphore_signal(barrier, inc=1, device_id=device, device_id_type=MESH)

    @pl.loop(0, PARTNERS)
    def _(i):
        other, _, _ = partner(i)
        for side in range(2):
            pl.semaphore_signal(
                barrier, inc=1, device_id=(other, n - core + side), device_id_type=MESH
            )

    row = lax.broadcasted_iota(jnp.int32, (TOK, TOK), 0)
    col = lax.broadcasted_iota(jnp.int32, (TOK, TOK), 1)
    order = (col == 8 * (row % 16) + row // 16).astype(F32).astype(BF16)
    loads[0].wait()
    unlike = (jnp.broadcast_to(ids_ref[...], (TOK, TOK)) != row % 16).astype(F32).astype(BF16)
    sorted_c = nt_dot(order, unlike)
    pc[...] = sorted_c.astype(BF16)
    lane16 = lanes_of((16, 128))
    low16 = lane16 < HDIM
    others = jnp.zeros((16, 128), F32)
    for residue in range(8):
        others = jnp.where(
            lane16 // 16 == residue, sorted_c[residue * 16:residue * 16 + 16], others
        )
    others = others.astype(BF16)
    for half in range(2):
        kv_sel[half, 0] = others
        q_sel[half, 0] = others

    def picked(source, a, shift):
        first = (2 * a + shift) % 8
        block = source[:, a * 128:(a + 1) * 128]
        return jnp.where(
            low16, block[first * 16:first * 16 + 16], block[first * 16 + 16:first * 16 + 32]
        ).astype(BF16)

    loads[1].wait()
    sorted_k = nn_dot(order, k_ref[...])
    pk[...] = sorted_k.astype(BF16)
    for a in range(6):
        for part in range(2):
            kv_sel[a // 3, 1 + 4 * (a % 3) + part] = picked(sorted_k, a, 4 * part)
    loads[2].wait()
    sorted_v = nn_dot(order, v_ref[...])
    pv[...] = sorted_v.astype(BF16)
    for a in range(6):
        for part in range(2):
            kv_sel[a // 3, 3 + 4 * (a % 3) + part] = picked(sorted_v, a, 4 * part)
    kv[core] = kv_sel[core]
    loads[3].wait()
    sorted_q = nn_dot(order, q_ref[...]) * (HDIM ** -0.5)
    pq[...] = sorted_q.astype(BF16)
    for a in range(6):
        for part in range(2):
            q_sel[a // 3, 1 + 3 * part + a % 3] = picked(sorted_q, a, 4 * part)
    q_in[place, core] = q_sel[core]

    pl.semaphore_wait(barrier, 7 + 2 * PARTNERS)

    def send(source, target, sent, arrived, device):
        return pltpu.make_async_remote_copy(
            source, target, ring_send.at[sent], ring_recv.at[arrived],
            device_id=device, device_id_type=MESH,
        )

    def pair_kv(part):
        first, count = KV_PARTS[part]
        rows = pl.ds(first, count)
        return send(
            kv_sel.at[1 - core, rows], kv.at[core, rows], part, core * 3 + part, pair
        )

    def pair_kv_arrival(part):
        first, count = KV_PARTS[part]
        rows = pl.ds(first, count)
        other = 1 - core
        return send(kv_sel.at[core, rows], kv.at[other, rows], part, other * 3 + part, pair)

    def first_kv(way, part, side):
        first, count = KV_PARTS[part]
        rows = pl.ds(first, count)
        slot = (2, 14)[way] + core
        device = (g, lax.rem(n - core + (2, 14)[way], 16) + side)
        return send(
            kv_sel.at[side, rows], kv.at[slot, rows],
            3 + (way * 3 + part) * 2 + side, slot * 3 + part, device,
        )

    def first_arrival(way, part, side):
        first, count = KV_PARTS[part]
        rows = pl.ds(first, count)
        slot = (2, 14)[way] + side
        return send(
            kv_sel.at[0, rows], kv.at[slot, rows],
            3 + (way * 3 + part) * 2 + side, slot * 3 + part, pair,
        )

    def passed(kind, way, part):
        first, count = KV_PARTS[part]
        rows = pl.ds(first, count)
        at, to = (((2, 4), (4, 6), (4, 8)), ((14, 12), (12, 10), (13, 9)))[way][kind]
        slots = 1 if kind == 2 else 2
        device = ((right, right, right2), (left, left, left2))[way][kind]
        return send(
            kv.at[pl.ds(at, slots), rows], kv.at[pl.ds(to, slots), rows],
            15 + (kind * 2 + way) * 3 + part, to * 3 + part, device,
        )

    both_ways = [(part, way) for part in range(3) for way in range(2)]
    for part, way in both_ways:
        for side in range(2):
            first_kv(way, part, side).start()
        if way == 1:
            pair_kv(part).start()
    pair_q = pltpu.make_async_remote_copy(
        q_sel.at[1 - core], q_in.at[place, core], pair_send.at[0], pair_recv.at[0],
        device_id=pair, device_id_type=MESH,
    )
    pair_q.start()

    def pass_on(stage):
        for part, way in both_ways:
            if stage == 0:
                for side in range(2):
                    first_arrival(way, part, side).wait_recv()
                passed(0, way, part).start()
            else:
                passed(0, way, part).wait_recv()
                passed(1, way, part).start()
                passed(2, way, part).start()

    def q_copy(i, side, inside):
        other, other_at, _ = partner(i)
        if inside:
            source, target, arrived = q_sel.at[side], q_in.at[place, core], q_recv_in.at[place, core]
        else:
            slot = out_slot(place, other_at)
            source, target = q_sel.at[side, pl.ds(0, 4)], q_out.at[slot, core]
            arrived = q_recv_out.at[slot, core]
        return pltpu.make_async_remote_copy(
            source, target, q_send.at[2 * i + side], arrived,
            device_id=(other, n - core + side), device_id_type=MESH,
        )

    def for_partners(act):
        @pl.loop(0, PARTNERS)
        def _(i):
            _, _, same = partner(i)

            @pl.when(same)
            def _():
                for side in range(2):
                    act(i, side, True)

            @pl.when(jnp.logical_not(same))
            def _():
                for side in range(2):
                    act(i, side, False)

    for_partners(lambda i, side, inside: q_copy(i, side, inside).start())

    ones = jnp.ones((TOK, 128), BF16)
    lane128 = lanes_of((TOK, 128))
    own_slide = jnp.where(lane128 < 16, (sorted_c - 1.0) * PENALTY, 0.0).astype(BF16)
    wide_low = lanes_of((TOK, 128)) < HDIM

    def local_pair(a):
        cols = slice(a * 128, (a + 1) * 128)
        block = pq[:, cols].astype(F32)
        left_side = jnp.concatenate(
            [
                jnp.concatenate([jnp.where(wide_low, block, 0.0).astype(BF16), own_slide], 1),
                jnp.concatenate([jnp.where(wide_low, 0.0, block).astype(BF16), own_slide], 1),
            ],
            0,
        )
        scores = nt_dot(left_side, jnp.concatenate([pk[:, cols], pc[...]], 1))
        top = jnp.max(scores, axis=1, keepdims=True)
        weights = jnp.exp(scores - top).astype(BF16)
        summed = nn_dot(weights, jnp.concatenate([pv[:, cols], ones], 1))
        result = summed[:, :128] / summed[:, 128:]
        level = top + jnp.log(summed[:, 128:])
        loc_o[:, cols] = jnp.where(wide_low, result[:TOK], result[TOK:])
        loc_l[:, cols] = jnp.where(wide_low, level[:TOK], level[TOK:])

    local_pair(0)
    local_pair(1)
    pass_on(0)
    local_pair(2)
    local_pair(3)
    pass_on(1)
    local_pair(4)
    local_pair(5)

    pair_q.wait_recv()

    @pl.loop(0, PARTNERS)
    def _(i):
        other, other_at, same = partner(i)

        @pl.when(same)
        def _():
            for side in range(2):
                spot = q_in.at[other_at, side]
                pltpu.make_async_copy(spot, spot, q_recv_in.at[other_at, side]).wait()

        @pl.when(jnp.logical_not(same))
        def _():
            slot = out_slot(other_at, place)
            for side in range(2):
                spot = q_out.at[slot, side]
                pltpu.make_async_copy(spot, spot, q_recv_out.at[slot, side]).wait()

    for side in range(2):
        for slot in range(SEG):
            q_roll[slot, side] = pltpu.roll(q_in[slot, side, 0].astype(F32), 64, 1).astype(BF16)
    for part in range(3):
        pair_kv_arrival(part).wait_recv()
        for way in range(2):
            passed(1, way, part).wait_recv()
            passed(2, way, part).wait_recv()
    for slot in range(16):
        kv_roll[slot] = pltpu.roll(kv[slot, 0].astype(F32), 64, 1).astype(BF16)

    many = jnp.ones((256, 128), BF16)
    half_masks = [
        jnp.where(low16, 1.0, 0.0).astype(BF16), jnp.where(low16, 0.0, 1.0).astype(BF16)
    ]
    masks = []
    for head in range(6):
        residue = lax.rem(6 * core + head, 8)
        masks.append(jnp.where(lane16 // 16 == residue, PENALTY, 0.0).astype(BF16))

    def stacked(value):
        return value.reshape(-1, 128)

    def left_side(block, slides, head):
        return jnp.concatenate(
            [stacked(block * half_masks[head % 2]), stacked((slides - 1) * masks[head])], 1
        )

    def levels(top, totals):
        return jnp.where(top < -PENALTY / 2, ABSENT, top + jnp.log(totals))

    def in_pieces(level):
        high = level.astype(BF16).astype(F32)
        rest = level - high
        middle = rest.astype(BF16).astype(F32)
        last = rest - middle
        at = lax.rem(lanes_of(level.shape), 8)
        pieces = jnp.where(
            at == 0, high, jnp.where(at == 1, middle, jnp.where(at == 2, last, 0.0))
        )
        return pieces.astype(BF16)

    def keys_of(part, j):
        slides = kv_roll[...] if part else kv[:, 0]
        return jnp.concatenate([stacked(kv[:, 1 + part + 4 * j]), stacked(slides)], 1)

    def values_of(part, j):
        return jnp.concatenate([stacked(kv[:, 3 + part + 4 * j]), many], 1)

    def inside(first, count):
        rows = count * 32
        span = pl.ds(first, count)
        low = lanes_of((rows, 128)) < HDIM
        spot = lanes_of((rows, 128)) // 8
        stats = jnp.zeros((rows, 128), F32)
        slides, turned = q_in[span, :, 0], q_roll[span]
        for j in range(3):
            far_q, near_q = q_in[span, :, 1 + j], q_in[span, :, 4 + j]
            lhs = jnp.concatenate(
                [
                    left_side(far_q, slides, 2 * j), left_side(near_q, turned, 2 * j),
                    left_side(far_q, slides, 2 * j + 1), left_side(near_q, turned, 2 * j + 1),
                ],
                0,
            )
            far_s, near_s = nt_dot(lhs, keys_of(0, j)), nt_dot(lhs, keys_of(1, j))
            top = jnp.max(jnp.maximum(far_s, near_s), axis=1, keepdims=True)
            far_o = nn_dot(jnp.exp(far_s - top).astype(BF16), values_of(0, j))
            both = far_o + nn_dot(jnp.exp(near_s - top).astype(BF16), values_of(1, j))
            for part in range(2):
                outs = []
                for u in range(2):
                    start = (2 * u + part) * rows
                    total = both[start:start + rows]
                    if part == 0:
                        total = total + far_o[start:start + rows]
                    outs.append(total[:, :128] / total[:, 128:])
                    level = levels(top[start:start + rows], total[:, 128:])
                    stats = jnp.where(spot == 8 * part + 2 * j + u, level, stats)
                o_in[span, :, 1 + 3 * part + j] = (
                    jnp.where(low, outs[0], outs[1]).astype(BF16).reshape(count, 2, 16, 128)
                )
        o_in[span, :, 0] = in_pieces(stats).reshape(count, 2, 16, 128)

    def outside(first, count):
        rows = count * 32
        span = pl.ds(first, count)
        low = lanes_of((rows, 128)) < HDIM
        spot = lanes_of((rows, 128)) // 8
        stats = jnp.zeros((rows, 128), F32)
        slides = q_out[span, :, 0]
        for j in range(3):
            far_q = q_out[span, :, 1 + j]
            lhs = jnp.concatenate(
                [left_side(far_q, slides, 2 * j), left_side(far_q, slides, 2 * j + 1)], 0
            )
            far_s = nt_dot(lhs, keys_of(0, j))
            top = jnp.max(far_s, axis=1, keepdims=True)
            total = nn_dot(jnp.exp(far_s - top).astype(BF16), values_of(0, j))
            result = total[:, :128] / total[:, 128:]
            level = levels(top, total[:, 128:])
            for u in range(2):
                stats = jnp.where(spot == 2 * j + u, level[u * rows:(u + 1) * rows], stats)
            o_out[span, :, 1 + j] = (
                jnp.where(low, result[:rows], result[rows:]).astype(BF16).reshape(count, 2, 16, 128)
            )
        o_out[span, :, 0] = in_pieces(stats).reshape(count, 2, 16, 128)

    def back_in(at, side):
        return pltpu.make_async_remote_copy(
            o_in.at[at, side], r_in.at[place, core], o_send_in.at[at, side],
            o_recv_in.at[place, core],
            device_id=(g - place + at, n - core + side), device_id_type=MESH,
        )

    def back_out(slot, side):
        at = lax.rem(slot + (place < 7).astype(jnp.int32) + place + 1, SEG)
        away = jnp.where(at > place, -SEG, SEG)
        other = lax.rem(g - place + at + away + WIDE, WIDE)
        return pltpu.make_async_remote_copy(
            o_out.at[slot, side], r_out.at[out_slot(place, at), core], o_send_out.at[slot, side],
            o_recv_out.at[out_slot(place, at), core],
            device_id=(other, n - core + side), device_id_type=MESH,
        )

    def if_near(at, act):
        apart = jnp.abs(at - place)

        @pl.when(jnp.logical_and(apart > 0, apart <= REACH))
        def _():
            for side in range(2):
                act(at, side)

    def if_used(slot, act):
        @pl.when(jnp.logical_or(slot < 5, lax.rem(place, 7) == 0))
        def _():
            for side in range(2):
                act(slot, side)

    @pl.loop(0, 2)
    def _(chunk):
        outside(3 * chunk, 3)
        for k in range(3):
            if_used(3 * chunk + k, lambda slot, side: back_out(slot, side).start())

    @pl.loop(0, 4)
    def _(chunk):
        inside(2 * chunk, 2)
        for k in range(2):
            if_near(2 * chunk + k, lambda at, side: back_in(at, side).start())

    pair_o = pltpu.make_async_remote_copy(
        o_in.at[place, 1 - core], r_in.at[place, core], pair_send.at[1], pair_recv.at[1],
        device_id=pair, device_id_type=MESH,
    )
    pair_o.start()
    r_in[place, core] = o_in[place, core]
    att[...] = loc_o[...]

    @pl.loop(0, PARTNERS)
    def _(i):
        other, other_at, same = partner(i)

        @pl.when(same)
        def _():
            for side in range(2):
                spot = r_in.at[other_at, side]
                pltpu.make_async_copy(spot, spot, o_recv_in.at[other_at, side]).wait()

        @pl.when(jnp.logical_not(same))
        def _():
            slot = out_slot(other_at, place)
            for side in range(2):
                spot = r_out.at[slot, side]
                pltpu.make_async_copy(spot, spot, o_recv_out.at[slot, side]).wait()

    pair_o.wait_recv()

    e_row = lax.broadcasted_iota(jnp.int32, (128, 384), 0)
    e_col = lax.broadcasted_iota(jnp.int32, (128, 384), 1)
    to_far = jnp.where((e_row // 8 == e_col // 64) & (e_row % 8 < 3), 1.0, 0.0).astype(BF16)
    to_near = jnp.where((e_row // 8 == e_col // 64 + 8) & (e_row % 8 < 3), 1.0, 0.0).astype(BF16)
    for half in range(2):
        stats_i = r_in[:, half, 0].reshape(128, 128)
        stats_o = r_out[:, half, 0].reshape(96, 128)
        far_i = nn_dot(stats_i, to_far)
        near_i = nn_dot(stats_i, to_near)
        far_o = nn_dot(stats_o, to_far)
        for j in range(3):
            a = 3 * half + j
            lanes = slice(j * 128, (j + 1) * 128)
            cols = slice(a * 128, (a + 1) * 128)
            for part in range(2):
                r0 = (2 * a + 4 * part) % 8 * 16
                r1 = r0 + 16
                own_l = jnp.where(low16, loc_l[r0:r0 + 16, cols], loc_l[r1:r1 + 16, cols])
                own_o = jnp.where(low16, loc_o[r0:r0 + 16, cols], loc_o[r1:r1 + 16, cols])
                lev = (near_i if part else far_i)[:, lanes].reshape(8, 16, 128)
                val = r_in[:, half, 1 + 3 * part + j].astype(F32)
                if part == 0:
                    lev = jnp.concatenate([lev, far_o[:, lanes].reshape(6, 16, 128)], 0)
                    val = jnp.concatenate([val, r_out[:, half, 1 + j].astype(F32)], 0)
                top = jnp.maximum(jnp.max(lev, axis=0), own_l)
                scale = jnp.exp(lev - top[None])
                own_scale = jnp.exp(own_l - top)
                numer = jnp.sum(scale * val, axis=0) + own_scale * own_o
                denom = jnp.sum(scale, axis=0) + own_scale
                joined = numer / denom
                att[r0:r0 + 16, a * 128:a * 128 + 64] = joined[:, :64]
                att[r1:r1 + 16, a * 128 + 64:a * 128 + 128] = joined[:, 64:]

    back = (row == 8 * (col % 16) + col // 16).astype(F32).astype(BF16)
    attended = nn_dot(back, att[...].astype(BF16)).astype(BF16)
    loads[4].wait()
    out_ref[...] = nn_dot(attended, w_vmem[...]).astype(BF16)

    pair_q.wait_send()
    pair_o.wait_send()
    for part, way in both_ways:
        for side in range(2):
            first_kv(way, part, side).wait_send()
        if way == 1:
            pair_kv(part).wait_send()
        for kind in range(3):
            passed(kind, way, part).wait_send()
    for_partners(lambda i, side, inside: q_copy(i, side, inside).wait_send())

    @pl.loop(0, 6)
    def _(slot):
        if_used(slot, lambda slot, side: back_out(slot, side).wait_send())

    @pl.loop(0, SEG)
    def _(at):
        if_near(at, lambda at, side: back_in(at, side).wait_send())


def local(queries, keys, values, slide_ids, w_out):
    vmem = pl.BlockSpec(memory_space=pltpu.VMEM)
    dma = pltpu.SemaphoreType.DMA
    return pl.pallas_call(
        kernel,
        out_shape=jax.ShapeDtypeStruct((TOK, WIDTH), BF16),
        in_specs=[pl.BlockSpec(memory_space=pltpu.HBM)] * 5,
        out_specs=vmem,
        scratch_shapes=[
            pltpu.VMEM((TOK, WIDTH), BF16),
            pltpu.VMEM((TOK, WIDTH), BF16),
            pltpu.VMEM((TOK, WIDTH), BF16),
            pltpu.VMEM((1, TOK), jnp.int32),
            pltpu.VMEM((TOK, WIDTH), BF16),
            pltpu.VMEM((TOK, WIDTH), BF16),
            pltpu.VMEM((TOK, WIDTH), BF16),
            pltpu.VMEM((TOK, 128), BF16),
            pltpu.VMEM((2, 13, 16, 128), BF16),
            pltpu.VMEM((2, 7, 16, 128), BF16),
            pltpu.VMEM((16, 13, 16, 128), BF16),
            pltpu.VMEM((16, 16, 128), BF16),
            pltpu.VMEM((8, 2, 7, 16, 128), BF16),
            pltpu.VMEM((6, 2, 4, 16, 128), BF16),
            pltpu.VMEM((8, 2, 16, 128), BF16),
            pltpu.VMEM((8, 2, 7, 16, 128), BF16),
            pltpu.VMEM((6, 2, 4, 16, 128), BF16),
            pltpu.VMEM((8, 2, 7, 16, 128), BF16),
            pltpu.VMEM((6, 2, 4, 16, 128), BF16),
            pltpu.VMEM((TOK, WIDTH), F32),
            pltpu.VMEM((TOK, WIDTH), F32),
            pltpu.VMEM((TOK, WIDTH), F32),
            pltpu.VMEM((WIDTH, WIDTH), BF16),
            dma((5,)),
            dma((2,)),
            dma((2,)),
            dma((33,)),
            dma((48,)),
            dma((24,)),
            dma((8, 2)),
            dma((6, 2)),
            dma((8, 2)),
            dma((6, 2)),
            dma((8, 2)),
            dma((6, 2)),
        ],
        compiler_params=pltpu.CompilerParams(
            collective_id=0, has_side_effects=True, vmem_limit_bytes=(63 * 1024 + 512) * 1024
        ),
        name="dilated",
    )(queries, keys, values, slide_ids.reshape(1, TOK), w_out)


def solution(mesh):
    placed = (
        P(("wide", "narrow"), None),
        P(("wide", "narrow"), None),
        P(("wide", "narrow"), None),
        P(("wide", "narrow")),
        P(),
    )
    return jax.shard_map(
        local, mesh=mesh, in_specs=placed, out_specs=P(("wide", "narrow"), None), check_vma=False
    )
```

time: 53 us -> 43.9 us (0.83)
  the two profiles are of different devices: /device:TPU:1 before, /device:TPU:7 now
where the time goes in v2:
time: 43.9 us; the launch traced here: 43.8 us
  Pallas kernels  42.1 us (96%)
  local copies, waits for them, and re-layouts  1.62 us (4%)
    pallas_call x1, Pallas kernels, local(): pl.pallas_call(kernel, out_shape=jax.ShapeDtypeStruct((TOK, WIDTH), BF16)...  42.1 us
    unnamed x1, local copies, waits for them, and re-layouts  1.62 us

profile of v2, /device:TPU:7, one launch (start us, length us, event | category | flops | bytes accessed | tf_op | source)
XLA Modules:
  0.0 43.8 jit_solution(5341682023413143637)
XLA Ops:
  0.0 42.1 %dilated.1 = bf16[128,768]{1,0:T(8,128)(2,1)} custom-call(bf16[128,768]{1,0:T(8,128)(2,1)} %q_hbm.1, bf16[128,768]{1,0:T(8,128)(2,1)} %k_hbm.1, bf16[128,768]{1,0:T(8,128)(2,1)} %v_hbm.1, s32[1,128]{1,0:T(1,128)} %bitcast.1, bf16[768,768]{1,0:T(8,128)(2,1)} %w_hbm.1), custom_call_target="tpu_custom_call" | custom-call | tf_op jit(solution)/shard_map/dilated/pallas_call | solution.py:536
  42.1 1.6 %copy.7 = bf16[128,768]{1,0:T(8,128)(2,1)} copy(bf16[128,768]{1,0:T(8,128)(2,1)} %dilated.1) | data formatting | bytes 393216

commit v3 on v2

--- a/solution.py
+++ b/solution.py
@@ -19,7 +19,9 @@
 BF16 = jnp.bfloat16
 F32 = jnp.float32
 
-KV_PARTS = ((0, 5), (5, 4), (9, 4))
+KV_PARTS = ((0, 4), (4, 3), (7, 3), (10, 3))
+PARTS = len(KV_PARTS)
+SLOTS = 2
 
 
 def lanes_of(shape):
@@ -74,7 +76,7 @@
             ((ids_hbm, ids_ref), (k_hbm, k_ref), (v_hbm, v_ref), (q_hbm, q_ref), (w_hbm, w_vmem))
         )
     ]
-    for load in loads:
+    for load in loads[:4]:
         load.start()
 
     barrier = pltpu.get_barrier_semaphore()
@@ -83,13 +85,13 @@
     for device in (pair, right, left, right2, left2) + crossed:
         pl.semaphore_signal(barrier, inc=1, device_id=device, device_id_type=MESH)
 
-    @pl.loop(0, PARTNERS)
-    def _(i):
-        other, _, _ = partner(i)
-        for side in range(2):
-            pl.semaphore_signal(
-                barrier, inc=1, device_id=(other, n - core + side), device_id_type=MESH
-            )
+    for apart in range(-REACH, REACH + 1):
+        if apart:
+            for side in range(2):
+                pl.semaphore_signal(
+                    barrier, inc=1, device_id_type=MESH,
+                    device_id=(lax.rem(g + apart + WIDE, WIDE), n - core + side),
+                )
 
     row = lax.broadcasted_iota(jnp.int32, (TOK, TOK), 0)
     col = lax.broadcasted_iota(jnp.int32, (TOK, TOK), 1)
@@ -122,22 +124,14 @@
     pk[...] = sorted_k.astype(BF16)
     for a in range(6):
         for part in range(2):
-            kv_sel[a // 3, 1 + 4 * (a % 3) + part] = picked(sorted_k, a, 4 * part)
+            kv_sel[a // 3, 1 + 2 * (a % 3) + 6 * part] = picked(sorted_k, a, 4 * part)
     loads[2].wait()
     sorted_v = nn_dot(order, v_ref[...])
     pv[...] = sorted_v.astype(BF16)
     for a in range(6):
         for part in range(2):
-            kv_sel[a // 3, 3 + 4 * (a % 3) + part] = picked(sorted_v, a, 4 * part)
+            kv_sel[a // 3, 2 + 2 * (a % 3) + 6 * part] = picked(sorted_v, a, 4 * part)
     kv[core] = kv_sel[core]
-    loads[3].wait()
-    sorted_q = nn_dot(order, q_ref[...]) * (HDIM ** -0.5)
-    pq[...] = sorted_q.astype(BF16)
-    for a in range(6):
-        for part in range(2):
-            q_sel[a // 3, 1 + 3 * part + a % 3] = picked(sorted_q, a, 4 * part)
-    q_in[place, core] = q_sel[core]
-
     pl.semaphore_wait(barrier, 7 + 2 * PARTNERS)
 
     def send(source, target, sent, arrived, device):
@@ -150,14 +144,14 @@
         first, count = KV_PARTS[part]
         rows = pl.ds(first, count)
         return send(
-            kv_sel.at[1 - core, rows], kv.at[core, rows], part, core * 3 + part, pair
+            kv_sel.at[1 - core, rows], kv.at[core, rows], part, core * PARTS + part, pair
         )
 
     def pair_kv_arrival(part):
         first, count = KV_PARTS[part]
         rows = pl.ds(first, count)
         other = 1 - core
-        return send(kv_sel.at[core, rows], kv.at[other, rows], part, other * 3 + part, pair)
+        return send(kv_sel.at[core, rows], kv.at[other, rows], part, other * PARTS + part, pair)
 
     def first_kv(way, part, side):
         first, count = KV_PARTS[part]
@@ -166,7 +160,7 @@
         device = (g, lax.rem(n - core + (2, 14)[way], 16) + side)
         return send(
             kv_sel.at[side, rows], kv.at[slot, rows],
-            3 + (way * 3 + part) * 2 + side, slot * 3 + part, device,
+            PARTS + (way * PARTS + part) * 2 + side, slot * PARTS + part, device,
         )
 
     def first_arrival(way, part, side):
@@ -175,7 +169,7 @@
         slot = (2, 14)[way] + side
         return send(
             kv_sel.at[0, rows], kv.at[slot, rows],
-            3 + (way * 3 + part) * 2 + side, slot * 3 + part, pair,
+            PARTS + (way * PARTS + part) * 2 + side, slot * PARTS + part, pair,
         )
 
     def passed(kind, way, part):
@@ -186,15 +180,24 @@
         device = ((right, right, right2), (left, left, left2))[way][kind]
         return send(
             kv.at[pl.ds(at, slots), rows], kv.at[pl.ds(to, slots), rows],
-            15 + (kind * 2 + way) * 3 + part, to * 3 + part, device,
-        )
-
-    both_ways = [(part, way) for part in range(3) for way in range(2)]
+            5 * PARTS + (kind * 2 + way) * PARTS + part, to * PARTS + part, device,
+        )
+
+    both_ways = [(part, way) for part in range(PARTS) for way in range(2)]
     for part, way in both_ways:
         for side in range(2):
             first_kv(way, part, side).start()
         if way == 1:
             pair_kv(part).start()
+    loads[3].wait()
+    sorted_q = nn_dot(order, q_ref[...]) * (HDIM ** -0.5)
+    pq[...] = sorted_q.astype(BF16)
+    for a in range(6):
+        for part in range(2):
+            q_sel[a // 3, 1 + 3 * part + a % 3] = picked(sorted_q, a, 4 * part)
+    q_in[place, core] = q_sel[core]
+    loads[4].start()
+
     pair_q = pltpu.make_async_remote_copy(
         q_sel.at[1 - core], q_in.at[place, core], pair_send.at[0], pair_recv.at[0],
         device_id=pair, device_id_type=MESH,
@@ -297,13 +300,13 @@
     for side in range(2):
         for slot in range(SEG):
             q_roll[slot, side] = pltpu.roll(q_in[slot, side, 0].astype(F32), 64, 1).astype(BF16)
-    for part in range(3):
-        pair_kv_arrival(part).wait_recv()
-        for way in range(2):
-            passed(1, way, part).wait_recv()
-            passed(2, way, part).wait_recv()
-    for slot in range(16):
-        kv_roll[slot] = pltpu.roll(kv[slot, 0].astype(F32), 64, 1).astype(BF16)
+
+    def await_kv(parts):
+        for part in parts:
+            pair_kv_arrival(part).wait_recv()
+            for way in range(2):
+                passed(1, way, part).wait_recv()
+                passed(2, way, part).wait_recv()
 
     many = jnp.ones((256, 128), BF16)
     half_masks = [
@@ -338,10 +341,10 @@
 
     def keys_of(part, j):
         slides = kv_roll[...] if part else kv[:, 0]
-        return jnp.concatenate([stacked(kv[:, 1 + part + 4 * j]), stacked(slides)], 1)
+        return jnp.concatenate([stacked(kv[:, 1 + 6 * part + 2 * j]), stacked(slides)], 1)
 
     def values_of(part, j):
-        return jnp.concatenate([stacked(kv[:, 3 + part + 4 * j]), many], 1)
+        return jnp.concatenate([stacked(kv[:, 2 + 6 * part + 2 * j]), many], 1)
 
     def inside(first, count):
         rows = count * 32
@@ -433,17 +436,23 @@
             for side in range(2):
                 act(slot, side)
 
+    await_kv((0, 1))
+
     @pl.loop(0, 2)
     def _(chunk):
         outside(3 * chunk, 3)
         for k in range(3):
             if_used(3 * chunk + k, lambda slot, side: back_out(slot, side).start())
 
-    @pl.loop(0, 4)
+    for slot in range(16):
+        kv_roll[slot] = pltpu.roll(kv[slot, 0].astype(F32), 64, 1).astype(BF16)
+    await_kv((2, 3))
+
+    @pl.loop(0, SEG // SLOTS)
     def _(chunk):
-        inside(2 * chunk, 2)
-        for k in range(2):
-            if_near(2 * chunk + k, lambda at, side: back_in(at, side).start())
+        inside(SLOTS * chunk, SLOTS)
+        for k in range(SLOTS):
+            if_near(SLOTS * chunk + k, lambda at, side: back_in(at, side).start())
 
     pair_o = pltpu.make_async_remote_copy(
         o_in.at[place, 1 - core], r_in.at[place, core], pair_send.at[1], pair_recv.at[1],
@@ -452,6 +461,15 @@
     pair_o.start()
     r_in[place, core] = o_in[place, core]
     att[...] = loc_o[...]
+    pair_q.wait_send()
+    for part, way in both_ways:
+        for side in range(2):
+            first_kv(way, part, side).wait_send()
+        if way == 1:
+            pair_kv(part).wait_send()
+        for kind in range(3):
+            passed(kind, way, part).wait_send()
+    for_partners(lambda i, side, inside: q_copy(i, side, inside).wait_send())
 
     @pl.loop(0, PARTNERS)
     def _(i):
@@ -510,16 +528,7 @@
     loads[4].wait()
     out_ref[...] = nn_dot(attended, w_vmem[...]).astype(BF16)
 
-    pair_q.wait_send()
     pair_o.wait_send()
-    for part, way in both_ways:
-        for side in range(2):
-            first_kv(way, part, side).wait_send()
-        if way == 1:
-            pair_kv(part).wait_send()
-        for kind in range(3):
-            passed(kind, way, part).wait_send()
-    for_partners(lambda i, side, inside: q_copy(i, side, inside).wait_send())
 
     @pl.loop(0, 6)
     def _(slot):
@@ -565,8 +574,8 @@
             dma((5,)),
             dma((2,)),
             dma((2,)),
-            dma((33,)),
-            dma((48,)),
+            dma((11 * PARTS,)),
+            dma((16 * PARTS,)),
             dma((24,)),
             dma((8, 2)),
             dma((6, 2)),

time: 43.9 us -> 42.6 us (0.970); the launches traced: 43.8 us -> 41.9 us
  Pallas kernels: 42.1 us -> 40.3 us
    pallas_call x1, Pallas kernels: 42.1 us -> 40.3 us  [local(): pl.pallas_call(kernel, out_shape=jax.ShapeDtypeStruct((TOK, WIDTH), BF16)...]
where the time goes in v3:
time: 42.6 us; the launch traced here: 41.9 us
  Pallas kernels  40.3 us (95%)
  local copies, waits for them, and re-layouts  1.62 us (4%)
    pallas_call x1, Pallas kernels, local(): pl.pallas_call(kernel, out_shape=jax.ShapeDtypeStruct((TOK, WIDTH), BF16)...  40.3 us
    unnamed x1, local copies, waits for them, and re-layouts  1.62 us

profile of v3, /device:TPU:7, one launch (start us, length us, event | category | flops | bytes accessed | tf_op | source)
XLA Modules:
  0.0 41.9 jit_solution(14981227247776817283)
XLA Ops:
  0.0 40.3 %dilated.1 = bf16[128,768]{1,0:T(8,128)(2,1)} custom-call(bf16[128,768]{1,0:T(8,128)(2,1)} %q_hbm.1, bf16[128,768]{1,0:T(8,128)(2,1)} %k_hbm.1, bf16[128,768]{1,0:T(8,128)(2,1)} %v_hbm.1, s32[1,128]{1,0:T(1,128)} %bitcast.1, bf16[768,768]{1,0:T(8,128)(2,1)} %w_hbm.1), custom_call_target="tpu_custom_call" | custom-call | tf_op jit(solution)/shard_map/dilated/pallas_call | solution.py:545
  40.3 1.6 %copy.7 = bf16[128,768]{1,0:T(8,128)(2,1)} copy(bf16[128,768]{1,0:T(8,128)(2,1)} %dilated.1) | data formatting | bytes 393216

commit v4 on v3

--- a/solution.py
+++ b/solution.py
@@ -449,7 +449,8 @@
     await_kv((2, 3))
 
     @pl.loop(0, SEG // SLOTS)
-    def _(chunk):
+    def _(step):
+        chunk = lax.rem(step + place // SLOTS + 1, SEG // SLOTS)
         inside(SLOTS * chunk, SLOTS)
         for k in range(SLOTS):
             if_near(SLOTS * chunk + k, lambda at, side: back_in(at, side).start())
@@ -585,7 +586,7 @@
             dma((6, 2)),
         ],
         compiler_params=pltpu.CompilerParams(
-            collective_id=0, has_side_effects=True, vmem_limit_bytes=(63 * 1024 + 512) * 1024
+            collective_id=0, has_side_effects=True, vmem_limit_bytes=54960 * 1024
         ),
         name="dilated",
     )(queries, keys, values, slide_ids.reshape(1, TOK), w_out)

time: 42.6 us -> 41.2 us (0.967)
  Pallas kernels: 40.3 us -> 39.3 us
    pallas_call x1, Pallas kernels: 40.3 us -> 39.3 us  [local(): pl.pallas_call(kernel, out_shape=jax.ShapeDtypeStruct((TOK, WIDTH), BF16)...]
    unnamed x1 -> x3, local copies, waits for them, and re-layouts: 1.62 us -> 1.33 us
where the time goes in v4:
time: 41.2 us; the launch traced here: 40.6 us
  Pallas kernels  39.3 us (95%)
  local copies, waits for them, and re-layouts  1.33 us (3%)
    pallas_call x1, Pallas kernels, local(): pl.pallas_call(kernel, out_shape=jax.ShapeDtypeStruct((TOK, WIDTH), BF16)...  39.3 us
    unnamed x3, local copies, waits for them, and re-layouts  1.33 us

profile of v4, /device:TPU:7, one launch (start us, length us, event | category | flops | bytes accessed | tf_op | source)
XLA Modules:
  0.0 40.6 jit_solution(17963978412941072766)
XLA Ops:
  0.0 0.0 copy-start
  0.0 0.7 %copy-done = s32[128]{0:T(128)S(1)} copy-done((s32[128]{0:T(128)S(1)}, s32[128]{0:T(128)}, u32[]{:S(2)}) %copy-start) | copy-done | bytes 536
  0.7 39.3 %dilated.1 = bf16[128,768]{1,0:T(8,128)(2,1)S(1)} custom-call(bf16[128,768]{1,0:T(8,128)(2,1)} %q_hbm.1, bf16[128,768]{1,0:T(8,128)(2,1)} %k_hbm.1, bf16[128,768]{1,0:T(8,128)(2,1)} %v_hbm.1, s32[1,128]{1,0:T(1,128)S(1)} %bitcast.1, bf16[768,768]{1,0:T(8,128)(2,1)} %w_hbm.1), custom_call_target="tpu_custom_call" | custom-call | tf_op jit(solution)/shard_map/dilated/pallas_call | solution.py:546
  39.9 0.7 %copy.7 = bf16[128,768]{1,0:T(8,128)(2,1)} copy(bf16[128,768]{1,0:T(8,128)(2,1)S(1)} %dilated.1) | data formatting | bytes 393216
Async XLA Ops:
  0.0 0.7 %copy-start = (s32[128]{0:T(128)S(1)}, s32[128]{0:T(128)}, u32[]{:S(2)}) copy-start(s32[128]{0:T(128)} %param.8) | copy-start | bytes 1540

commit v5 on v4

--- a/solution.py
+++ b/solution.py
@@ -19,7 +19,7 @@
 BF16 = jnp.bfloat16
 F32 = jnp.float32
 
-KV_PARTS = ((0, 4), (4, 3), (7, 3), (10, 3))
+KV_PARTS = ((0, 7), (7, 6))
 PARTS = len(KV_PARTS)
 SLOTS = 2
 
@@ -63,21 +63,21 @@
         other = lax.rem(g + offset + WIDE, WIDE)
         return other, lax.rem(other, SEG), other // SEG == g // SEG
 
+    loads = [
+        pltpu.make_async_copy(source, target, in_sem.at[at])
+        for at, (source, target) in enumerate(
+            ((ids_hbm, ids_ref), (k_hbm, k_ref), (v_hbm, v_ref), (q_hbm, q_ref), (w_hbm, w_vmem))
+        )
+    ]
+    for load in loads[:4]:
+        load.start()
+
     empty = jnp.where(lax.rem(lanes_of((2, 16, 128)), 8) == 0, ABSENT, 0.0).astype(BF16)
     spare = SEG - 1 - place
     r_in[spare] = jnp.zeros((2, 7, 16, 128), BF16)
     r_in[spare, :, 0] = empty
     r_out[5] = jnp.zeros((2, 4, 16, 128), BF16)
     r_out[5, :, 0] = empty
-
-    loads = [
-        pltpu.make_async_copy(source, target, in_sem.at[at])
-        for at, (source, target) in enumerate(
-            ((ids_hbm, ids_ref), (k_hbm, k_ref), (v_hbm, v_ref), (q_hbm, q_ref), (w_hbm, w_vmem))
-        )
-    ]
-    for load in loads[:4]:
-        load.start()
 
     barrier = pltpu.get_barrier_semaphore()
     turn = 1 - 2 * core
@@ -436,17 +436,17 @@
             for side in range(2):
                 act(slot, side)
 
-    await_kv((0, 1))
-
-    @pl.loop(0, 2)
-    def _(chunk):
-        outside(3 * chunk, 3)
-        for k in range(3):
-            if_used(3 * chunk + k, lambda slot, side: back_out(slot, side).start())
+    await_kv((0,))
+
+    outside(0, 6)
+
+    @pl.loop(0, 6)
+    def _(slot):
+        if_used(slot, lambda slot, side: back_out(slot, side).start())
 
     for slot in range(16):
         kv_roll[slot] = pltpu.roll(kv[slot, 0].astype(F32), 64, 1).astype(BF16)
-    await_kv((2, 3))
+    await_kv((1,))
 
     @pl.loop(0, SEG // SLOTS)
     def _(step):
@@ -471,6 +471,16 @@
         for kind in range(3):
             passed(kind, way, part).wait_send()
     for_partners(lambda i, side, inside: q_copy(i, side, inside).wait_send())
+
+    pair_o.wait_send()
+
+    @pl.loop(0, 6)
+    def _(slot):
+        if_used(slot, lambda slot, side: back_out(slot, side).wait_send())
+
+    @pl.loop(0, SEG)
+    def _(at):
+        if_near(at, lambda at, side: back_in(at, side).wait_send())
 
     @pl.loop(0, PARTNERS)
     def _(i):
@@ -528,16 +538,6 @@
     attended = nn_dot(back, att[...].astype(BF16)).astype(BF16)
     loads[4].wait()
     out_ref[...] = nn_dot(attended, w_vmem[...]).astype(BF16)
-
-    pair_o.wait_send()
-
-    @pl.loop(0, 6)
-    def _(slot):
-        if_used(slot, lambda slot, side: back_out(slot, side).wait_send())
-
-    @pl.loop(0, SEG)
-    def _(at):
-        if_near(at, lambda at, side: back_in(at, side).wait_send())
 
 
 def local(queries, keys, values, slide_ids, w_out):

time: 41.2 us -> 40.8 us (level)
  no operation moved by 1% of the time
where the time goes in v5:
time: 40.8 us; the launch traced here: 40.6 us
  Pallas kernels  39.2 us (96%)
  local copies, waits for them, and re-layouts  1.33 us (3%)
    pallas_call x1, Pallas kernels, local(): pl.pallas_call(kernel, out_shape=jax.ShapeDtypeStruct((TOK, WIDTH), BF16)...  39.2 us
    unnamed x3, local copies, waits for them, and re-layouts  1.33 us

profile of v5, /device:TPU:7, one launch (start us, length us, event | category | flops | bytes accessed | tf_op | source)
XLA Modules:
  0.0 40.6 jit_solution(4429867826752215048)
XLA Ops:
  0.0 0.0 copy-start
  0.0 0.7 %copy-done = s32[128]{0:T(128)S(1)} copy-done((s32[128]{0:T(128)S(1)}, s32[128]{0:T(128)}, u32[]{:S(2)}) %copy-start) | copy-done | bytes 536
  0.7 39.2 %dilated.1 = bf16[128,768]{1,0:T(8,128)(2,1)S(1)} custom-call(bf16[128,768]{1,0:T(8,128)(2,1)} %q_hbm.1, bf16[128,768]{1,0:T(8,128)(2,1)} %k_hbm.1, bf16[128,768]{1,0:T(8,128)(2,1)} %v_hbm.1, s32[1,128]{1,0:T(1,128)S(1)} %bitcast.1, bf16[768,768]{1,0:T(8,128)(2,1)} %w_hbm.1), custom_call_target="tpu_custom_call" | custom-call | tf_op jit(solution)/shard_map/dilated/pallas_call | solution.py:546
  39.9 0.7 %copy.7 = bf16[128,768]{1,0:T(8,128)(2,1)} copy(bf16[128,768]{1,0:T(8,128)(2,1)S(1)} %dilated.1) | data formatting | bytes 393216
Async XLA Ops:
  0.0 0.7 %copy-start = (s32[128]{0:T(128)S(1)}, s32[128]{0:T(128)}, u32[]{:S(2)}) copy-start(s32[128]{0:T(128)} %param.8) | copy-start | bytes 1540

commit v6 on v5

--- a/solution.py
+++ b/solution.py
@@ -19,7 +19,7 @@
 BF16 = jnp.bfloat16
 F32 = jnp.float32
 
-KV_PARTS = ((0, 7), (7, 6))
+KV_PARTS = ((0, 4), (4, 3), (7, 3), (10, 3))
 PARTS = len(KV_PARTS)
 SLOTS = 2
 
@@ -436,7 +436,7 @@
             for side in range(2):
                 act(slot, side)
 
-    await_kv((0,))
+    await_kv((0, 1))
 
     outside(0, 6)
 
@@ -446,7 +446,7 @@
 
     for slot in range(16):
         kv_roll[slot] = pltpu.roll(kv[slot, 0].astype(F32), 64, 1).astype(BF16)
-    await_kv((1,))
+    await_kv((2, 3))
 
     @pl.loop(0, SEG // SLOTS)
     def _(step):

time: 40.8 us -> 40.4 us (level)
  no operation moved by 1% of the time
where the time goes in v6:
time: 40.4 us; the launch traced here: 40.3 us
  Pallas kernels  39 us (97%)
  local copies, waits for them, and re-layouts  1.33 us (3%)
    pallas_call x1, Pallas kernels, local(): pl.pallas_call(kernel, out_shape=jax.ShapeDtypeStruct((TOK, WIDTH), BF16)...  39 us
    unnamed x3, local copies, waits for them, and re-layouts  1.33 us

profile of v6, /device:TPU:7, one launch (start us, length us, event | category | flops | bytes accessed | tf_op | source)
XLA Modules:
  0.0 40.3 jit_solution(14663104226173607302)
XLA Ops:
  0.0 0.0 copy-start
  0.0 0.7 %copy-done = s32[128]{0:T(128)S(1)} copy-done((s32[128]{0:T(128)S(1)}, s32[128]{0:T(128)}, u32[]{:S(2)}) %copy-start) | copy-done | bytes 536
  0.7 39.0 %dilated.1 = bf16[128,768]{1,0:T(8,128)(2,1)S(1)} custom-call(bf16[128,768]{1,0:T(8,128)(2,1)} %q_hbm.1, bf16[128,768]{1,0:T(8,128)(2,1)} %k_hbm.1, bf16[128,768]{1,0:T(8,128)(2,1)} %v_hbm.1, s32[1,128]{1,0:T(1,128)S(1)} %bitcast.1, bf16[768,768]{1,0:T(8,128)(2,1)} %w_hbm.1), custom_call_target="tpu_custom_call" | custom-call | tf_op jit(solution)/shard_map/dilated/pallas_call | solution.py:546
  39.6 0.7 %copy.7 = bf16[128,768]{1,0:T(8,128)(2,1)} copy(bf16[128,768]{1,0:T(8,128)(2,1)S(1)} %dilated.1) | data formatting | bytes 393216
Async XLA Ops:
  0.0 0.7 %copy-start = (s32[128]{0:T(128)S(1)}, s32[128]{0:T(128)}, u32[]{:S(2)}) copy-start(s32[128]{0:T(128)} %param.8) | copy-start | bytes 1540

commit v7 on v6

--- a/solution.py
+++ b/solution.py
@@ -19,7 +19,7 @@
 BF16 = jnp.bfloat16
 F32 = jnp.float32
 
-KV_PARTS = ((0, 4), (4, 3), (7, 3), (10, 3))
+KV_PARTS = ((0, 4), (4, 3), (7, 6))
 PARTS = len(KV_PARTS)
 SLOTS = 2
 
@@ -446,7 +446,7 @@
 
     for slot in range(16):
         kv_roll[slot] = pltpu.roll(kv[slot, 0].astype(F32), 64, 1).astype(BF16)
-    await_kv((2, 3))
+    await_kv((2,))
 
     @pl.loop(0, SEG // SLOTS)
     def _(step):

time: 40.4 us -> 40 us (0.990)
  Pallas kernels: 39 us -> 38.5 us
    pallas_call x1, Pallas kernels: 39 us -> 38.5 us  [local(): pl.pallas_call(kernel, out_shape=jax.ShapeDtypeStruct((TOK, WIDTH), BF16)...]
where the time goes in v7:
time: 40 us; the launch traced here: 39.8 us
  Pallas kernels  38.5 us (96%)
  local copies, waits for them, and re-layouts  1.33 us (3%)
    pallas_call x1, Pallas kernels, local(): pl.pallas_call(kernel, out_shape=jax.ShapeDtypeStruct((TOK, WIDTH), BF16)...  38.5 us
    unnamed x3, local copies, waits for them, and re-layouts  1.33 us

profile of v7, /device:TPU:7, one launch (start us, length us, event | category | flops | bytes accessed | tf_op | source)
XLA Modules:
  0.0 39.8 jit_solution(17836751736782552208)
XLA Ops:
  0.0 0.0 copy-start
  0.0 0.7 %copy-done = s32[128]{0:T(128)S(1)} copy-done((s32[128]{0:T(128)S(1)}, s32[128]{0:T(128)}, u32[]{:S(2)}) %copy-start) | copy-done | bytes 536
  0.7 38.5 %dilated.1 = bf16[128,768]{1,0:T(8,128)(2,1)S(1)} custom-call(bf16[128,768]{1,0:T(8,128)(2,1)} %q_hbm.1, bf16[128,768]{1,0:T(8,128)(2,1)} %k_hbm.1, bf16[128,768]{1,0:T(8,128)(2,1)} %v_hbm.1, s32[1,128]{1,0:T(1,128)S(1)} %bitcast.1, bf16[768,768]{1,0:T(8,128)(2,1)} %w_hbm.1), custom_call_target="tpu_custom_call" | custom-call | tf_op jit(solution)/shard_map/dilated/pallas_call | solution.py:546
  39.1 0.7 %copy.7 = bf16[128,768]{1,0:T(8,128)(2,1)} copy(bf16[128,768]{1,0:T(8,128)(2,1)S(1)} %dilated.1) | data formatting | bytes 393216
Async XLA Ops:
  0.0 0.7 %copy-start = (s32[128]{0:T(128)S(1)}, s32[128]{0:T(128)}, u32[]{:S(2)}) copy-start(s32[128]{0:T(128)} %param.8) | copy-start | bytes 1540
